TPU v7x, 256 devices: a whole 4x4x8 slice. The times are simulated.
256 devices in a mesh: dp: 64 (over x, z, core), mp: 4 (over y).
Axes of the slice: x: 4, y: 4, z: 8, core: 2. Of those that a mesh axis runs over, the one named last changes fastest.
Arguments:
- grads: bfloat16 [4096, 14336], P('dp', 'mp'), may hold values from -6 to 6
- second_moment: float32 [4096, 14336], P('dp', 'mp'), may hold values from 0.02 to 4
- owners: int32 [4, 56], P('mp'), may hold values from 0 to 63, as said below
- stats_left: float32 [4, 128, 512, 512], P('mp', 'dp'), as said below
- stats_right: float32 [4, 128, 512, 512], P('mp', 'dp'), as said below
- root_left: bfloat16 [4, 128, 512, 512], P('mp', 'dp'), as said below
- root_right: bfloat16 [4, 128, 512, 512], P('mp', 'dp'), as said below
Outputs:
- direction: bfloat16 [4096, 14336], P('dp', 'mp')
- new_moment: float32 [4096, 14336], P('dp', 'mp')
- new_left: float32 [4, 128, 512, 512], P('mp', 'dp')
- new_right: float32 [4, 128, 512, 512], P('mp', 'dp')
Inputs may be any that keep to these rules, and one draw needn't show every extreme that they name: In each row of owners no value appears more than 2 times, and in every row some value appears exactly 2 times. `stats_left`: Symmetric. `stats_right`: Symmetric. `root_left`: Symmetric. `root_right`: Symmetric.
All inputs are finite; a program needn't handle non-finite values.
Results may differ from a plain program's by a relative error of at most 0.0054.
Values may be sent and summed in bfloat16 or wider, within the bound.
No kernel may reach another device: no remote copies, remote signals or barrier semaphores. Data moves between devices by JAX's collectives and lax.ppermute only.
A program may use at most 64 MiB of HBM per device.

v0:
```python
import jax
import jax.numpy as jnp
from jax import lax
from jax.sharding import PartitionSpec as P

stat_decay = 0.9
moment_decay = 0.99
adam_epsilon = 1e-08
norm_epsilon = 1e-06


def per_device(grads, second_moment, owners, stats_left, stats_right, root_left, root_right):
    rows_dev, col_width = grads.shape
    block_size = stats_left.shape[2]
    capacity = stats_left.shape[1]
    col_blocks = col_width // block_size
    owner_count = lax.axis_size("dp")
    my_index = lax.axis_index("dp")
    piece = block_size // owner_count
    row_blocks = rows_dev // piece
    coef = (1.0 - stat_decay) / block_size
    owner = owners[0]
    n_blocks = owner.shape[0]
    block_ids = jnp.arange(n_blocks, dtype=jnp.int32)
    earlier = (owner[:, None] == owner[None, :]) & (block_ids[None, :] < block_ids[:, None])
    slot_of = jnp.sum(earlier.astype(jnp.int32), axis=1)
    owner_hot = owner[:, None] == jnp.arange(owner_count, dtype=jnp.int32)[None, :]
    slot_hot = slot_of[:, None] == jnp.arange(capacity, dtype=jnp.int32)[None, :]
    selector = (owner_hot[:, :, None] & slot_hot[:, None, :]).astype(jnp.float32).transpose(1, 2, 0)
    selector_half = selector.astype(jnp.bfloat16)
    local_blocks = grads.reshape(row_blocks, piece, col_blocks, block_size).transpose(0, 2, 1, 3)
    local_blocks = local_blocks.reshape(n_blocks, piece, block_size)
    outgoing = jnp.einsum(
        "osb,brk->osrk", selector_half, local_blocks, preferred_element_type=jnp.float32
    ).astype(jnp.bfloat16)
    grad_wide = grads.astype(jnp.float32)
    new_moment = moment_decay * second_moment + (1.0 - moment_decay) * grad_wide * grad_wide
    adam = grad_wide / (jnp.sqrt(new_moment) + adam_epsilon)
    block_sq = jnp.sum(
        (adam * adam).reshape(row_blocks, piece, col_blocks, block_size), axis=(1, 3)
    ).reshape(n_blocks)
    arrived = lax.all_to_all(outgoing, "dp", split_axis=0, concat_axis=0, tiled=True)
    totals = lax.psum(block_sq, "dp")
    mine_hot = ((owner == my_index)[:, None] & slot_hot).astype(jnp.float32)
    slot_sq = jnp.sum(mine_hot * totals[:, None], axis=0)
    slot_grads = arrived.transpose(1, 0, 2, 3).reshape(capacity, block_size, block_size)
    left_applied = jnp.einsum(
        "sij,sjk->sik", root_left[0], slot_grads, preferred_element_type=jnp.float32
    ).astype(jnp.bfloat16)
    precond = jnp.einsum(
        "sij,sjk->sik", left_applied, root_right[0], preferred_element_type=jnp.float32
    )
    graft_scale = jnp.sqrt(slot_sq) / jnp.sqrt(
        jnp.sum(precond * precond, axis=(1, 2)) + norm_epsilon
    )
    directions = (graft_scale[:, None, None] * precond).astype(jnp.bfloat16)
    reply_buf = directions.reshape(capacity, owner_count, piece, block_size).transpose(1, 0, 2, 3)
    returned = lax.all_to_all(reply_buf, "dp", split_axis=0, concat_axis=0, tiled=True)
    placed = jnp.einsum(
        "osb,osrk->brk", selector_half, returned, preferred_element_type=jnp.float32
    )
    placed = placed.astype(jnp.bfloat16).reshape(row_blocks, col_blocks, piece, block_size)
    direction = placed.transpose(0, 2, 1, 3).reshape(rows_dev, col_width)
    gram_left = jnp.einsum(
        "sik,sjk->sij", slot_grads, slot_grads, preferred_element_type=jnp.float32
    )
    gram_right = jnp.einsum(
        "ski,skj->sij", slot_grads, slot_grads, preferred_element_type=jnp.float32
    )
    new_left = stat_decay * stats_left[0] + coef * gram_left
    new_right = stat_decay * stats_right[0] + coef * gram_right
    return (direction, new_moment, new_left[None], new_right[None])


def solution(mesh):
    in_specs = (
        P("dp", "mp"),
        P("dp", "mp"),
        P("mp", None),
        P("mp", "dp", None, None),
        P("mp", "dp", None, None),
        P("mp", "dp", None, None),
        P("mp", "dp", None, None),
    )
    out_specs = (P("dp", "mp"), P("dp", "mp"), P("mp", "dp", None, None), P("mp", "dp", None, None))
    return jax.shard_map(
        per_device, mesh=mesh, in_specs=in_specs, out_specs=out_specs, check_vma=False
    )
```

profile of v0, /device:TPU:1, one launch (start us, length us, event | category | flops | bytes accessed | tf_op | source)
XLA Modules:
  0.0 204.2 jit_solution(3297878520632686668)
XLA Ops:
  0.6 0.0 copy-start
  0.6 0.9 convert_reduce_fusion
  1.6 0.7 iota_compare_fusion.1
  2.3 1.6 convolution_convert_fusion
  3.9 0.0 copy-start.2
  3.9 1.5 copy.30
  5.5 13.0 %all-to-all-start = ((bf16[64,2,8,512]{3,2,1,0:T(8,128)(2,1)}), bf16[64,2,8,512]{3,2,1,0:T(8,128)(2,1)S(1)}, u32[]{:S(2)}, u32[]{:S(2)}) async-start(bf16[64,2,8,512]{3,2,1,0:T(8,128)(2,1)} %copy.30), calls=%async_computation | async-start | bytes 2097152 | tf_op jit(solution)/shard_map/all_to_all | solution.py:42
  18.5 0.0 copy-start.3
  18.5 0.0 copy-done.2
  18.5 2.6 %fusion.13 = (f32[64,3584]{1,0:T(8,128)S(1)}, f32[64,3584]{1,0:T(8,128)}) fusion(bf16[64,3584]{1,0:T(8,128)(2,1)S(1)} %copy-done.2, f32[64,3584]{1,0:T(8,128)} %param.8), kind=kLoop, calls=%fused_computation.21 | loop fusion | flops 1835008 | bytes 3211264 | tf_op jit(solution)/shard_map/mul | solution.py:40
  21.1 0.2 reduce_sum.37
  21.2 0.1 reshape.92
  21.3 139.7 %psum.7 = f32[56]{0:T(128)S(1)} all-reduce(f32[56]{0:T(128)S(1)} %reshape.92), channel_id=1, replica_groups=mesh['dp'=64,'mp'=4] {'dp'}, use_global_device_ids=true, to_apply=%region_2.0 | all-reduce | flops 56 | bytes 448 | tf_op jit(solution)/shard_map/psum | solution.py:43
  161.0 0.0 copy-done.3
  161.0 0.1 fusion.30
  161.1 0.0 all-to-all-done
  161.1 0.0 copy-done
  161.1 4.0 %multiply_reduce_fusion = (f32[2]{0:T(128)S(1)}, f32[2,512,512]{2,1,0:T(8,128)}) fusion(bf16[1,2,512,512]{3,2,1,0:T(8,128)(2,1)S(1)} %copy-done, bf16[1,2,512,512]{3,2,1,0:T(8,128)(2,1)} %param.12, bf16[64,2,8,512]{3,2,1,0:T(8,128)(2,1)S(1)} %all-to-all-done), kind=kOutput, calls=%fused_computation.5 | convolution fusion | flops 1075314688 | bytes 5242888 | tf_op jit(solution)/shard_map/sij,sjk->sik/dot_general | solution.py:50
  165.1 1.9 fusion.4
  167.0 2.1 %copy.65 = bf16[2,64,8,512]{3,0,2,1:T(2,128)(2,1)} copy(bf16[2,64,8,512]{3,2,1,0:T(8,128)(2,1)S(1)} %fusion.4) | data formatting | bytes 2097152 | tf_op jit(solution)/shard_map/reshape | solution.py:57
  169.1 4.3 %all-to-all-start.1 = ((bf16[64,2,8,512]{3,1,2,0:T(2,128)(2,1)}), bf16[64,2,8,512]{3,1,2,0:T(2,128)(2,1)S(1)}, u32[]{:S(2)}, u32[]{:S(2)}) async-start(bf16[64,2,8,512]{3,1,2,0:T(2,128)(2,1)} %bitcast.68), calls=%async_computation.1 | async-start | bytes 2097152 | tf_op jit(solution)/shard_map/all_to_all | solution.py:58
  173.4 0.0 copy-start.1
  173.4 3.9 %fusion = f32[1,2,512,512]{3,2,1,0:T(8,128)} fusion(f32[1,2,512,512]{3,2,1,0:T(8,128)} %param.11, bf16[64,2,8,512]{3,2,1,0:T(8,128)(2,1)S(1)} %all-to-all-done), kind=kOutput, calls=%fused_computation.1 | convolution fusion | flops 538443776 | bytes 5242880 | tf_op jit(solution)/shard_map/ski,skj->sij/dot_general | solution.py:67
  177.3 0.0 copy-done.1
  177.3 2.2 %fusion.1 = f32[1,2,512,512]{3,2,1,0:T(8,128)} fusion(f32[1,2,512,512]{3,2,1,0:T(8,128)S(1)} %copy-done.1, bf16[64,2,8,512]{3,2,1,0:T(8,128)(2,1)S(1)} %all-to-all-done), kind=kOutput, calls=%fused_computation.3 | convolution fusion | flops 538443776 | bytes 5242880 | tf_op jit(solution)/shard_map/sik,sjk->sij/dot_general | solution.py:64
  179.5 22.5 %all-to-all-done.1 = bf16[64,2,8,512]{3,1,2,0:T(2,128)(2,1)S(1)} async-done(((bf16[64,2,8,512]{3,1,2,0:T(2,128)(2,1)}), bf16[64,2,8,512]{3,1,2,0:T(2,128)(2,1)S(1)}, u32[]{:S(2)}, u32[]{:S(2)}) %all-to-all-start.1) | async-done | bytes 1048608 | tf_op jit(solution)/shard_map/all_to_all | solution.py:58
  202.0 1.3 fusion.3
  203.3 0.9 copy.36
  (3 shorter events, 0.0 us)
Async XLA Ops:
  0.6 160.5 %copy-start = (bf16[1,2,512,512]{3,2,1,0:T(8,128)(2,1)S(1)}, bf16[1,2,512,512]{3,2,1,0:T(8,128)(2,1)}, u32[]{:S(2)}) copy-start(bf16[1,2,512,512]{3,2,1,0:T(8,128)(2,1)} %param.13) | copy-start | bytes 3145732
  3.9 14.6 %copy-start.2 = (bf16[64,3584]{1,0:T(8,128)(2,1)S(1)}, bf16[64,3584]{1,0:T(8,128)(2,1)}, u32[]{:S(2)}) copy-start(bf16[64,3584]{1,0:T(8,128)(2,1)} %param.7) | copy-start | bytes 1376260
  5.5 155.6 %all-to-all-start = ((bf16[64,2,8,512]{3,2,1,0:T(8,128)(2,1)}), bf16[64,2,8,512]{3,2,1,0:T(8,128)(2,1)S(1)}, u32[]{:S(2)}, u32[]{:S(2)}) async-start(bf16[64,2,8,512]{3,2,1,0:T(8,128)(2,1)} %copy.30), calls=%async_computation | async-start | bytes 2097152 | tf_op jit(solution)/shard_map/all_to_all | solution.py:42
  18.5 142.5 %copy-start.3 = (s32[1,56]{1,0:T(1,128)S(1)}, s32[1,56]{1,0:T(1,128)}, u32[]{:S(2)}) copy-start(s32[1,56]{1,0:T(1,128)} %param.9) | copy-start | bytes 676
  169.1 32.9 %all-to-all-start.1 = ((bf16[64,2,8,512]{3,1,2,0:T(2,128)(2,1)}), bf16[64,2,8,512]{3,1,2,0:T(2,128)(2,1)S(1)}, u32[]{:S(2)}, u32[]{:S(2)}) async-start(bf16[64,2,8,512]{3,1,2,0:T(2,128)(2,1)} %bitcast.68), calls=%async_computation.1 | async-start | bytes 2097152 | tf_op jit(solution)/shard_map/all_to_all | solution.py:58
  173.4 3.9 %copy-start.1 = (f32[1,2,512,512]{3,2,1,0:T(8,128)S(1)}, f32[1,2,512,512]{3,2,1,0:T(8,128)}, u32[]{:S(2)}) copy-start(f32[1,2,512,512]{3,2,1,0:T(8,128)} %param.10) | copy-start | bytes 6291460
where the time goes:
time: 205 us; the launch traced here: 204 us
  blocking collectives  140 us (68%)
  waiting for transfers between devices  22.5 us (11%)
  starting transfers between devices  17.3 us (8%)
  matrix products  12.9 us (6%)
  other arithmetic  6.46 us (3%)
  local copies, waits for them, and re-layouts  4.64 us (2%)
    psum x1, blocking collectives, per_device(): totals = lax.psum(block_sq, 'dp')  140 us
    all_to_all x1, waiting for transfers between devices, per_device(): lax.all_to_all(reply_buf, 'dp', split_axis=0, concat_axis=0, tiled=True)  22.5 us
    all_to_all x1, starting transfers between devices, per_device(): lax.all_to_all(outgoing, 'dp', split_axis=0, concat_axis=0, tiled=True)  13 us
    all_to_all x1, starting transfers between devices, per_device(): lax.all_to_all(reply_buf, 'dp', split_axis=0, concat_axis=0, tiled=True)  4.31 us
  transfers between devices with their start and end apart: 2, of which 1 were waited for; matrix products, arithmetic and copies ran while one was open for 4% of the time, Pallas kernels for 0%

commit v1 on v0

v1 whole, which is shorter than its diff:
```python
import functools

import jax
import jax.numpy as jnp
from jax import lax
from jax.experimental import pallas as pl
from jax.experimental.pallas import tpu as pltpu
from jax.sharding import PartitionSpec as P

stat_decay = 0.9
moment_decay = 0.99
adam_epsilon = 1e-08
norm_epsilon = 1e-06
LANES = 128
VMEM_BYTES = 58 * 1024 * 1024


def route_kernel(piece, tiles, col_blocks, n_blocks, owner_ref, me_ref, grads_hbm, out_ref, where_ref, mine_ref, count, grads_ref, sem):
    fetch = pltpu.make_async_copy(grads_hbm, grads_ref, sem)
    fetch.start()
    owner_count = out_ref.shape[0]
    capacity = mine_ref.shape[0]
    me = me_ref[0]
    for o in range(owner_count):
        count[o] = 0
    for s in range(capacity):
        mine_ref[s] = -1
    for b in range(n_blocks):
        o = owner_ref[0, b]
        s = count[o]
        count[o] = s + 1
        where_ref[0, b] = o
        where_ref[1, b] = s

        @pl.when(o == me)
        def _():
            mine_ref[s] = b

    fetch.wait()
    row_blocks = n_blocks // col_blocks
    for r in range(0, row_blocks, 2):
        for c in range(col_blocks):
            wide = grads_ref[r * piece:(r + 2) * piece, c * tiles * LANES:(c + 1) * tiles * LANES]
            wide = wide.astype(jnp.float32)
            for half in range(2):
                b = (r + half) * col_blocks + c
                o = where_ref[0, b]
                s = where_ref[1, b]
                part = wide[half * piece:(half + 1) * piece].astype(jnp.bfloat16)
                for j in range(tiles):
                    out_ref[o, s * tiles + j] = part[:, j * LANES:(j + 1) * LANES]


def apply_kernel(tiles, mine_ref, sums_ref, arrived_hbm, left_hbm, right_hbm, reply_hbm, slots_hbm,
                 arrived, left, right, reply, slots, tail, in_sems, out_sems):
    capacity, owner_count, _, piece, _ = arrived.shape
    size = left.shape[1]
    loads = []
    for s in range(capacity):
        loads.append((
            pltpu.make_async_copy(arrived_hbm.at[:, pl.ds(s * tiles, tiles)], arrived.at[s], in_sems.at[s, 0]),
            pltpu.make_async_copy(left_hbm.at[s], left.at[s], in_sems.at[s, 1]),
            pltpu.make_async_copy(right_hbm.at[s], right.at[s], in_sems.at[s, 2]),
        ))
    for copies in loads:
        for copy in copies:
            copy.start()
    tail[...] = jnp.broadcast_to(sums_ref[...][None], tail.shape)
    stores = [pltpu.make_async_copy(tail, reply_hbm.at[:, capacity * tiles], out_sems.at[0])]
    stores[-1].start()
    for s in range(capacity):
        loads[s][0].wait()
        cols = [arrived[s, :, j].astype(jnp.float32).reshape(size, LANES) for j in range(tiles)]
        grad = jnp.concatenate(cols, axis=1)
        grad = jnp.where(mine_ref[s] >= 0, grad, 0.0).astype(jnp.bfloat16)
        slots[s] = grad
        stores.append(pltpu.make_async_copy(slots.at[s], slots_hbm.at[s], out_sems.at[1 + s]))
        stores[-1].start()
        loads[s][1].wait()
        applied = jnp.dot(left[s], grad, preferred_element_type=jnp.float32).astype(jnp.bfloat16)
        loads[s][2].wait()
        precond = jnp.dot(applied, right[s], preferred_element_type=jnp.float32)
        total = jnp.sum(precond * precond, keepdims=True)
        unit = precond * (1.0 / jnp.sqrt(total + norm_epsilon))
        for j in range(tiles):
            part = unit[:, j * LANES:(j + 1) * LANES].reshape(owner_count, piece, LANES)
            reply[s, :, j] = part.astype(jnp.bfloat16)
        stores.append(pltpu.make_async_copy(reply.at[s], reply_hbm.at[:, pl.ds(s * tiles, tiles)], out_sems.at[1 + capacity + s]))
        stores[-1].start()
    for copy in stores:
        copy.wait()


def place_kernel(piece, tiles, col_blocks, n_blocks, where_ref, back_ref, out_ref):
    sums = jnp.sum(back_ref[:, back_ref.shape[1] - 1].astype(jnp.float32), axis=0)
    sums = sums + pltpu.roll(sums, LANES // 2, 1)
    root = jnp.sqrt(sums)
    row_blocks = n_blocks // col_blocks
    for r in range(0, row_blocks, 2):
        for c in range(col_blocks):
            found = []
            for half in range(2):
                b = (r + half) * col_blocks + c
                found.append((where_ref[0, b], where_ref[1, b], jnp.broadcast_to(root[:, b:b + 1], (piece, LANES))))
            for j in range(tiles):
                parts = [back_ref[o, s * tiles + j].astype(jnp.float32) * scale for o, s, scale in found]
                both = jnp.concatenate(parts, axis=0).astype(jnp.bfloat16)
                start = (c * tiles + j) * LANES
                out_ref[r * piece:(r + 2) * piece, start:start + LANES] = both


def params():
    return pltpu.CompilerParams(vmem_limit_bytes=VMEM_BYTES)


def per_device(grads, second_moment, owners, stats_left, stats_right, root_left, root_right):
    rows_dev, col_width = grads.shape
    block_size = stats_left.shape[2]
    capacity = stats_left.shape[1]
    col_blocks = col_width // block_size
    owner_count = lax.axis_size("dp")
    piece = block_size // owner_count
    row_blocks = rows_dev // piece
    n_blocks = row_blocks * col_blocks
    tiles = block_size // LANES
    coef = (1.0 - stat_decay) / block_size
    me = lax.axis_index("dp").astype(jnp.int32).reshape(1)
    smem = pl.BlockSpec(memory_space=pltpu.SMEM)
    vmem = pl.BlockSpec(memory_space=pltpu.VMEM)
    hbm = pl.BlockSpec(memory_space=pl.ANY)

    outgoing, where, mine = pl.pallas_call(
        functools.partial(route_kernel, piece, tiles, col_blocks, n_blocks),
        out_shape=(
            jax.ShapeDtypeStruct((owner_count, capacity * tiles, piece, LANES), jnp.bfloat16),
            jax.ShapeDtypeStruct((2, n_blocks), jnp.int32),
            jax.ShapeDtypeStruct((capacity,), jnp.int32),
        ),
        in_specs=[smem, smem, hbm],
        out_specs=(vmem, smem, smem),
        scratch_shapes=[
            pltpu.SMEM((owner_count,), jnp.int32),
            pltpu.VMEM((rows_dev, col_width), jnp.bfloat16),
            pltpu.SemaphoreType.DMA(()),
        ],
        compiler_params=params(),
        name="route",
    )(owners, me, grads)
    arrived = lax.all_to_all(outgoing, "dp", split_axis=0, concat_axis=0, tiled=True)

    grad_wide = grads.astype(jnp.float32)
    new_moment = moment_decay * second_moment + (1.0 - moment_decay) * grad_wide * grad_wide
    adam = grad_wide / (jnp.sqrt(new_moment) + adam_epsilon)
    block_sq = jnp.sum(
        (adam * adam).reshape(row_blocks, piece, col_blocks, block_size), axis=(1, 3)
    ).reshape(n_blocks)
    high = block_sq.astype(jnp.bfloat16)
    low = (block_sq - high.astype(jnp.float32)).astype(jnp.bfloat16)
    pad = jnp.zeros((LANES // 2 - n_blocks,), jnp.bfloat16)
    sums = jnp.broadcast_to(jnp.concatenate([high, pad, low, pad])[None], (piece, LANES))

    reply, slot_grads = pl.pallas_call(
        functools.partial(apply_kernel, tiles),
        out_shape=(
            jax.ShapeDtypeStruct((owner_count, capacity * tiles + 1, piece, LANES), jnp.bfloat16),
            jax.ShapeDtypeStruct((capacity, block_size, block_size), jnp.bfloat16),
        ),
        in_specs=[smem, vmem, hbm, hbm, hbm],
        out_specs=(hbm, hbm),
        scratch_shapes=[
            pltpu.VMEM((capacity, owner_count, tiles, piece, LANES), jnp.bfloat16),
            pltpu.VMEM((capacity, block_size, block_size), jnp.bfloat16),
            pltpu.VMEM((capacity, block_size, block_size), jnp.bfloat16),
            pltpu.VMEM((capacity, owner_count, tiles, piece, LANES), jnp.bfloat16),
            pltpu.VMEM((capacity, block_size, block_size), jnp.bfloat16),
            pltpu.VMEM((owner_count, piece, LANES), jnp.bfloat16),
            pltpu.SemaphoreType.DMA((capacity, 3)),
            pltpu.SemaphoreType.DMA((1 + 2 * capacity,)),
        ],
        compiler_params=params(),
        name="apply",
    )(mine, sums, arrived, root_left[0], root_right[0])
    returned = lax.all_to_all(reply, "dp", split_axis=0, concat_axis=0, tiled=True)

    gram_left = jnp.einsum("sik,sjk->sij", slot_grads, slot_grads, preferred_element_type=jnp.float32)
    gram_right = jnp.einsum("ski,skj->sij", slot_grads, slot_grads, preferred_element_type=jnp.float32)
    new_left = stat_decay * stats_left[0] + coef * gram_left
    new_right = stat_decay * stats_right[0] + coef * gram_right

    direction = pl.pallas_call(
        functools.partial(place_kernel, piece, tiles, col_blocks, n_blocks),
        out_shape=jax.ShapeDtypeStruct((rows_dev, col_width), jnp.bfloat16),
        in_specs=[smem, vmem],
        out_specs=vmem,
        compiler_params=params(),
        name="place",
    )(where, returned)
    return (direction, new_moment, new_left[None], new_right[None])


def solution(mesh):
    in_specs = (
        P("dp", "mp"),
        P("dp", "mp"),
        P("mp", None),
        P("mp", "dp", None, None),
        P("mp", "dp", None, None),
        P("mp", "dp", None, None),
        P("mp", "dp", None, None),
    )
    out_specs = (P("dp", "mp"), P("dp", "mp"), P("mp", "dp", None, None), P("mp", "dp", None, None))
    return jax.shard_map(
        per_device, mesh=mesh, in_specs=in_specs, out_specs=out_specs, check_vma=False
    )
```

time: 205 us -> 93.1 us (0.45)
  blocking collectives: 140 us -> 0 us
  waiting for transfers between devices: 22.5 us -> 52.2 us
  Pallas kernels: 0 us -> 10.8 us
  matrix products: 12.9 us -> 5.99 us
  other arithmetic: 6.46 us -> 1.65 us
  local copies, waits for them, and re-layouts: 4.64 us -> 2.09 us
    psum x1 -> x0, blocking collectives: 140 us -> none  [per_device(): totals = lax.psum(block_sq, 'dp')]
    all_to_all x1, waiting for transfers between devices: 0.01 us -> 26.8 us  [per_device(): lax.all_to_all(outgoing, 'dp', split_axis=0, concat_axis=0, tiled=True)]
    pallas_call x0 -> x3, Pallas kernels: none -> 10.8 us  [the longest x1 5.55 us: per_device(): pl.pallas_call(functools.partial(apply_kernel, tiles), out_shape=(jax.Sha...]
    dot_general x3 -> x0, matrix products: 6.87 us -> none  [the longest x1 3.99 us: per_device(): jnp.einsum('sij,sjk->sik', left_applied, root_right[0], preferred_element...]
    all_to_all x1, waiting for transfers between devices: 22.5 us -> 25.4 us  [per_device(): lax.all_to_all(reply, 'dp', split_axis=0, concat_axis=0, tiled=True)]
    convert_element_type x2 -> x0, local copies, waits for them, and re-layouts: 2.46 us -> none  [the longest x1 1.55 us: per_device(): outgoing = jnp.einsum('osb,brk->osrk', selector_half, local_blocks, prefe...]
    reshape x1 -> x0, local copies, waits for them, and re-layouts: 2.07 us -> none  [per_device(): directions.reshape(capacity, owner_count, piece, block_size)]
  transfers between devices with their start and end apart: 2 -> 2, of which waited for: 1 -> 2; matrix products, arithmetic and copies ran while one was open for 4% -> 8% of each run, Pallas kernels for 0% -> 0%
where the time goes in v1:
time: 93.1 us; the launch traced here: 92.8 us
  waiting for transfers between devices  52.2 us (56%)
  starting transfers between devices  19.3 us (21%)
  Pallas kernels  10.8 us (12%)
  matrix products  5.99 us (6%)
  local copies, waits for them, and re-layouts  2.09 us (2%)
  other arithmetic  1.65 us (2%)
    all_to_all x1, waiting for transfers between devices, per_device(): lax.all_to_all(outgoing, 'dp', split_axis=0, concat_axis=0, tiled=True)  26.8 us
    all_to_all x1, waiting for transfers between devices, per_device(): lax.all_to_all(reply, 'dp', split_axis=0, concat_axis=0, tiled=True)  25.4 us
    all_to_all x1, starting transfers between devices, per_device(): lax.all_to_all(outgoing, 'dp', split_axis=0, concat_axis=0, tiled=True)  13 us
    all_to_all x1, starting transfers between devices, per_device(): lax.all_to_all(reply, 'dp', split_axis=0, concat_axis=0, tiled=True)  6.33 us
    pallas_call x1, Pallas kernels, per_device(): pl.pallas_call(functools.partial(apply_kernel, tiles), out_shape=(jax.Sha...  5.55 us
    dot_general x1, matrix products, per_device(): jnp.einsum('ski,skj->sij', slot_grads, slot_grads, preferred_element_type...  3.9 us
    pallas_call x1, Pallas kernels, per_device(): pl.pallas_call(functools.partial(route_kernel, piece, tiles, col_blocks,...  2.91 us
    pallas_call x1, Pallas kernels, per_device(): pl.pallas_call(functools.partial(place_kernel, piece, tiles, col_blocks,...  2.37 us
  transfers between devices with their start and end apart: 2, of which 2 were waited for; matrix products, arithmetic and copies ran while one was open for 8% of the time, Pallas kernels for 0%

profile of v1, /device:TPU:1, one launch (start us, length us, event | category | flops | bytes accessed | tf_op | source)
XLA Modules:
  0.0 92.8 jit_solution(9311115899187187848)
XLA Ops:
  0.6 0.0 copy-start.4
  0.6 0.0 copy-start.5
  0.7 2.9 %route.1 = (bf16[64,8,8,128]{3,2,1,0:T(8,128)(2,1)}, s32[2,56]{1,0:T(2,128)}, s32[2]{0:T(128)}) custom-call(s32[1,56]{1,0:T(1,128)} %owner_ref.1, s32[1]{0:T(128)} %bitcast.me_ref, bf16[64,3584]{1,0:T(8,128)(2,1)} %grads_hbm.1), custom_call_target="tpu_custom_call" | custom-call | tf_op jit(solution)/shard_map/route/pallas_call | solution.py:132
  3.6 13.0 %all-to-all-start = ((bf16[64,8,8,128]{3,2,1,0:T(8,128)(2,1)}), bf16[64,8,8,128]{3,2,1,0:T(8,128)(2,1)S(1)}, u32[]{:S(2)}, u32[]{:S(2)}) async-start(bf16[64,8,8,128]{3,2,1,0:T(8,128)(2,1)} %get-tuple-element.11), calls=%async_computation | async-start | bytes 2097152 | tf_op jit(solution)/shard_map/all_to_all | solution.py:149
  16.6 0.0 copy-done.4
  16.6 0.0 copy-done.5
  16.6 1.4 %fusion.2 = (f32[64,3584]{1,0:T(8,128)S(1)}, f32[64,3584]{1,0:T(8,128)}) fusion(bf16[64,3584]{1,0:T(8,128)(2,1)S(1)} %copy-done.4, f32[64,3584]{1,0:T(8,128)S(1)} %copy-done.5), kind=kLoop, calls=%fused_computation.6 | loop fusion | flops 1835008 | bytes 3211264 | tf_op jit(solution)/shard_map/mul | solution.py:155
  18.0 0.2 reduce_sum.9
  18.2 0.1 reshape.24
  18.3 0.1 pad_maximum_fusion
  18.3 26.8 %all-to-all-done.arrived_hbm = bf16[64,8,8,128]{3,2,1,0:T(8,128)(2,1)S(1)} async-done(((bf16[64,8,8,128]{3,2,1,0:T(8,128)(2,1)}), bf16[64,8,8,128]{3,2,1,0:T(8,128)(2,1)S(1)}, u32[]{:S(2)}, u32[]{:S(2)}) %all-to-all-start) | async-done | bytes 1048608 | tf_op jit(solution)/shard_map/all_to_all | solution.py:149
  45.1 0.0 copy-start.2
  45.1 0.6 broadcast_in_dim.12.sums_ref
  45.8 0.4 copy-done.2
  46.1 5.6 %apply.1 = (bf16[64,9,8,128]{3,2,1,0:T(8,128)(2,1)}, bf16[2,512,512]{2,1,0:T(8,128)(2,1)}) custom-call(s32[2]{0:T(128)} %get-tuple-element.10.mine_ref, bf16[8,128]{1,0:T(8,128)(2,1)} %broadcast_in_dim.12.sums_ref, bf16[64,8,8,128]{3,2,1,0:T(8,128)(2,1)} %copy-done.2, bf16[2,512,512]{2,1,0:T(8,128)(2,1)} %bitcast.21, bf16[2,512,512]{2,1,0:T(8,128)(2,1)} %bitcast.22), custom_call_target="tpu_custom_call" | custom-call | tf_op jit(solution)/shard_map/apply/pallas_call | solution.py:162
  51.7 0.0 copy-start
  51.7 6.3 %all-to-all-start.1 = ((bf16[64,9,8,128]{3,2,1,0:T(8,128)(2,1)}), bf16[64,9,8,128]{3,2,1,0:T(8,128)(2,1)S(1)}, u32[]{:S(2)}, u32[]{:S(2)}) async-start(bf16[64,9,8,128]{3,2,1,0:T(8,128)(2,1)} %get-tuple-element.12), calls=%async_computation.1 | async-start | bytes 2359296 | tf_op jit(solution)/shard_map/all_to_all | solution.py:183
  58.0 0.0 copy-done
  58.0 0.0 copy-start.3
  58.0 3.9 %fusion = f32[1,2,512,512]{3,2,1,0:T(8,128)} fusion(f32[1,2,512,512]{3,2,1,0:T(8,128)} %param.11, bf16[2,512,512]{2,1,0:T(8,128)(2,1)S(1)} %copy-done), kind=kOutput, calls=%fused_computation.1 | convolution fusion | flops 538443776 | bytes 5242880 | tf_op jit(solution)/shard_map/ski,skj->sij/dot_general | solution.py:186
  61.9 0.0 copy-done.3
  61.9 2.1 %fusion.1 = f32[1,2,512,512]{3,2,1,0:T(8,128)} fusion(f32[1,2,512,512]{3,2,1,0:T(8,128)S(1)} %copy-done.3, bf16[2,512,512]{2,1,0:T(8,128)(2,1)S(1)} %copy-done), kind=kOutput, calls=%fused_computation.3 | convolution fusion | flops 538443776 | bytes 5242880 | tf_op jit(solution)/shard_map/sik,sjk->sij/dot_general | solution.py:185
  64.0 25.4 %all-to-all-done.1.back_ref = bf16[64,9,8,128]{3,2,1,0:T(8,128)(2,1)S(1)} async-done(((bf16[64,9,8,128]{3,2,1,0:T(8,128)(2,1)}), bf16[64,9,8,128]{3,2,1,0:T(8,128)(2,1)S(1)}, u32[]{:S(2)}, u32[]{:S(2)}) %all-to-all-start.1) | async-done | bytes 1179680 | tf_op jit(solution)/shard_map/all_to_all | solution.py:183
  89.4 0.0 copy-start.1
  89.4 1.0 %copy-done.1 = bf16[64,9,8,128]{3,2,1,0:T(8,128)(2,1)} copy-done((bf16[64,9,8,128]{3,2,1,0:T(8,128)(2,1)}, bf16[64,9,8,128]{3,2,1,0:T(8,128)(2,1)S(1)}, u32[]{:S(2)}) %copy-start.1) | copy-done | bytes 1179672
  90.4 2.4 %place.1 = bf16[64,3584]{1,0:T(8,128)(2,1)} custom-call(s32[2,56]{1,0:T(2,128)} %get-tuple-element.9.where_ref, bf16[64,9,8,128]{3,2,1,0:T(8,128)(2,1)} %copy-done.1), custom_call_target="tpu_custom_call" | custom-call | tf_op jit(solution)/shard_map/place/pallas_call | solution.py:190
  (2 shorter events, 0.0 us)
Async XLA Ops:
  0.6 15.9 %copy-start.4 = (bf16[64,3584]{1,0:T(8,128)(2,1)S(1)}, bf16[64,3584]{1,0:T(8,128)(2,1)}, u32[]{:S(2)}) copy-start(bf16[64,3584]{1,0:T(8,128)(2,1)} %grads_hbm.1) | copy-start | bytes 1376260
  0.6 15.9 %copy-start.5 = (f32[64,3584]{1,0:T(8,128)S(1)}, f32[64,3584]{1,0:T(8,128)}, u32[]{:S(2)}) copy-start(f32[64,3584]{1,0:T(8,128)} %param.8) | copy-start | bytes 2752516
  3.6 41.6 %all-to-all-start = ((bf16[64,8,8,128]{3,2,1,0:T(8,128)(2,1)}), bf16[64,8,8,128]{3,2,1,0:T(8,128)(2,1)S(1)}, u32[]{:S(2)}, u32[]{:S(2)}) async-start(bf16[64,8,8,128]{3,2,1,0:T(8,128)(2,1)} %get-tuple-element.11), calls=%async_computation | async-start | bytes 2097152 | tf_op jit(solution)/shard_map/all_to_all | solution.py:149
  45.1 1.0 %copy-start.2 = (bf16[64,8,8,128]{3,2,1,0:T(8,128)(2,1)}, bf16[64,8,8,128]{3,2,1,0:T(8,128)(2,1)S(1)}, u32[]{:S(2)}) copy-start(bf16[64,8,8,128]{3,2,1,0:T(8,128)(2,1)S(1)} %all-to-all-done.arrived_hbm) | copy-start | bytes 3145732
  51.7 6.4 %copy-start = (bf16[2,512,512]{2,1,0:T(8,128)(2,1)S(1)}, bf16[2,512,512]{2,1,0:T(8,128)(2,1)}, u32[]{:S(2)}) copy-start(bf16[2,512,512]{2,1,0:T(8,128)(2,1)} %get-tuple-element.13) | copy-start | bytes 3145732
  51.7 37.7 %all-to-all-start.1 = ((bf16[64,9,8,128]{3,2,1,0:T(8,128)(2,1)}), bf16[64,9,8,128]{3,2,1,0:T(8,128)(2,1)S(1)}, u32[]{:S(2)}, u32[]{:S(2)}) async-start(bf16[64,9,8,128]{3,2,1,0:T(8,128)(2,1)} %get-tuple-element.12), calls=%async_computation.1 | async-start | bytes 2359296 | tf_op jit(solution)/shard_map/all_to_all | solution.py:183
  58.0 3.9 %copy-start.3 = (f32[1,2,512,512]{3,2,1,0:T(8,128)S(1)}, f32[1,2,512,512]{3,2,1,0:T(8,128)}, u32[]{:S(2)}) copy-start(f32[1,2,512,512]{3,2,1,0:T(8,128)} %param.10) | copy-start | bytes 6291460
  89.4 1.0 %copy-start.1 = (bf16[64,9,8,128]{3,2,1,0:T(8,128)(2,1)}, bf16[64,9,8,128]{3,2,1,0:T(8,128)(2,1)S(1)}, u32[]{:S(2)}) copy-start(bf16[64,9,8,128]{3,2,1,0:T(8,128)(2,1)S(1)} %all-to-all-done.1.back_ref) | copy-start | bytes 3538948

commit v2 on v1

v2 whole, which is shorter than its diff:
```python
import functools

import jax
import jax.numpy as jnp
from jax import lax
from jax.experimental import pallas as pl
from jax.experimental.pallas import tpu as pltpu
from jax.sharding import PartitionSpec as P

stat_decay = 0.9
moment_decay = 0.99
adam_epsilon = 1e-08
norm_epsilon = 1e-06
LANES = 128
VMEM_BYTES = 12 * 1024 * 1024
VMEM_WHOLE = 58 * 1024 * 1024


def route_kernel(piece, tiles, col_blocks, n_blocks, owner_hbm, grads_hbm, out_ref, where_ref, mine_ref, owner_ref, count, grads_ref, sems):
    listing = pltpu.make_async_copy(owner_hbm, owner_ref, sems.at[0])
    listing.start()
    fetch = pltpu.make_async_copy(grads_hbm, grads_ref, sems.at[1])
    fetch.start()
    owner_count = out_ref.shape[0]
    capacity = mine_ref.shape[0]
    me = lax.axis_index("dp")
    for o in range(owner_count):
        count[o] = 0
    for s in range(capacity):
        mine_ref[s] = -1
    listing.wait()
    for b in range(n_blocks):
        o = owner_ref[0, b]
        s = count[o]
        count[o] = s + 1
        where_ref[0, b] = o
        where_ref[1, b] = s

        @pl.when(o == me)
        def _():
            mine_ref[s] = b

    fetch.wait()
    row_blocks = n_blocks // col_blocks
    for r in range(0, row_blocks, 2):
        for c in range(col_blocks):
            wide = grads_ref[r * piece:(r + 2) * piece, c * tiles * LANES:(c + 1) * tiles * LANES]
            wide = wide.astype(jnp.float32)
            for half in range(2):
                b = (r + half) * col_blocks + c
                o = where_ref[0, b]
                s = where_ref[1, b]
                part = wide[half * piece:(half + 1) * piece].astype(jnp.bfloat16)
                for j in range(tiles):
                    out_ref[o, s * tiles + j] = part[:, j * LANES:(j + 1) * LANES]


def apply_kernel(tiles, mine_ref, arrived, left_hbm, right_hbm, reply_hbm, slots, left, right, reply, sems):
    owner_count, _, piece, _ = arrived.shape
    capacity, size, _ = slots.shape
    loads = []
    for s in range(capacity):
        loads.append(pltpu.make_async_copy(left_hbm.at[s], left.at[s], sems.at[0, s]))
        loads.append(pltpu.make_async_copy(right_hbm.at[s], right.at[s], sems.at[1, s]))
    for load in loads:
        load.start()
    def gather(s):
        cols = [arrived[:, s * tiles + j].astype(jnp.float32).reshape(size, LANES) for j in range(tiles)]
        grad = jnp.concatenate(cols, axis=1)
        slots[s] = jnp.where(mine_ref[s] >= 0, grad, 0.0).astype(jnp.bfloat16)

    def first(s):
        return jnp.dot(left[s], slots[s], preferred_element_type=jnp.float32).astype(jnp.bfloat16)

    def second(s, applied):
        return jnp.dot(applied, right[s], preferred_element_type=jnp.float32)

    def send(s, precond):
        total = jnp.sum(precond * precond, keepdims=True)
        unit = precond * (1.0 / jnp.sqrt(total + norm_epsilon))
        for j in range(tiles):
            part = unit[:, j * LANES:(j + 1) * LANES].reshape(owner_count, piece, LANES)
            reply[s, :, j] = part.astype(jnp.bfloat16)
        store = pltpu.make_async_copy(reply.at[s], reply_hbm.at[:, pl.ds(s * tiles, tiles)], sems.at[2, s])
        store.start()
        return store

    stores = []
    gather(0)
    loads[0].wait()
    applied = first(0)
    for s in range(1, capacity):
        gather(s)
    for load in loads[1:]:
        load.wait()
    for s in range(capacity):
        precond = second(s, applied)
        if s + 1 < capacity:
            applied = first(s + 1)
        stores.append(send(s, precond))
    for store in stores:
        store.wait()


def place_kernel(piece, tiles, col_blocks, n_blocks, where_ref, sums_ref, back_ref, out_hbm, out_ref, sems):
    root = jnp.sqrt(sums_ref[...])
    row_blocks = n_blocks // col_blocks
    stores = []
    for r in range(0, row_blocks, 2):
        rows = pl.ds(r * piece, 2 * piece)
        for c in range(col_blocks):
            found = []
            for half in range(2):
                b = (r + half) * col_blocks + c
                found.append((where_ref[0, b], where_ref[1, b], jnp.broadcast_to(root[:, b:b + 1], (piece, LANES))))
            for j in range(tiles):
                parts = [back_ref[o, s * tiles + j].astype(jnp.float32) * scale for o, s, scale in found]
                both = jnp.concatenate(parts, axis=0).astype(jnp.bfloat16)
                start = (c * tiles + j) * LANES
                out_ref[r * piece:(r + 2) * piece, start:start + LANES] = both
        stores.append(pltpu.make_async_copy(out_ref.at[rows], out_hbm.at[rows], sems.at[r // 2]))
        stores[-1].start()
    for store in stores:
        store.wait()


def swap(value, step):
    pairs = [(i, i ^ step) for i in range(lax.axis_size("dp"))]
    return lax.ppermute(value, "dp", pairs)


def params(limit=VMEM_BYTES):
    return pltpu.CompilerParams(vmem_limit_bytes=limit)


def per_device(grads, second_moment, owners, stats_left, stats_right, root_left, root_right):
    rows_dev, col_width = grads.shape
    block_size = stats_left.shape[2]
    capacity = stats_left.shape[1]
    col_blocks = col_width // block_size
    owner_count = lax.axis_size("dp")
    piece = block_size // owner_count
    row_blocks = rows_dev // piece
    n_blocks = row_blocks * col_blocks
    tiles = block_size // LANES
    coef = (1.0 - stat_decay) / block_size
    smem = pl.BlockSpec(memory_space=pltpu.SMEM)
    vmem = pl.BlockSpec(memory_space=pltpu.VMEM)
    hbm = pl.BlockSpec(memory_space=pl.ANY)

    outgoing, where, mine = pl.pallas_call(
        functools.partial(route_kernel, piece, tiles, col_blocks, n_blocks),
        out_shape=(
            jax.ShapeDtypeStruct((owner_count, capacity * tiles, piece, LANES), jnp.bfloat16),
            jax.ShapeDtypeStruct((2, n_blocks), jnp.int32),
            jax.ShapeDtypeStruct((capacity,), jnp.int32),
        ),
        in_specs=[hbm, hbm],
        out_specs=(vmem, smem, smem),
        scratch_shapes=[
            pltpu.SMEM((1, n_blocks), jnp.int32),
            pltpu.SMEM((owner_count,), jnp.int32),
            pltpu.VMEM((rows_dev, col_width), jnp.bfloat16),
            pltpu.SemaphoreType.DMA((2,)),
        ],
        compiler_params=params(VMEM_WHOLE),
        name="route",
    )(owners, grads)
    arrived = lax.all_to_all(outgoing, "dp", split_axis=0, concat_axis=0, tiled=True)

    grad_wide = grads.astype(jnp.float32)
    new_moment = moment_decay * second_moment + (1.0 - moment_decay) * grad_wide * grad_wide
    adam = grad_wide / (jnp.sqrt(new_moment) + adam_epsilon)
    block_sq = jnp.sum(
        (adam * adam).reshape(row_blocks, piece, col_blocks, block_size), axis=(1, 3)
    ).reshape(n_blocks)
    sums = block_sq.reshape(1, n_blocks)
    for step in (1, 16, 32):
        sums = sums + swap(sums, step)
    sums = sums + swap(sums, 2) + swap(sums, 4) + swap(sums, 6)

    arrived, sums = lax.optimization_barrier((arrived, sums))
    reply, slot_grads = pl.pallas_call(
        functools.partial(apply_kernel, tiles),
        out_shape=(
            jax.ShapeDtypeStruct((owner_count, capacity * tiles, piece, LANES), jnp.bfloat16),
            jax.ShapeDtypeStruct((capacity, block_size, block_size), jnp.bfloat16),
        ),
        in_specs=[smem, vmem, hbm, hbm],
        out_specs=(hbm, vmem),
        scratch_shapes=[
            pltpu.VMEM((capacity, block_size, block_size), jnp.bfloat16),
            pltpu.VMEM((capacity, block_size, block_size), jnp.bfloat16),
            pltpu.VMEM((capacity, owner_count, tiles, piece, LANES), jnp.bfloat16),
            pltpu.SemaphoreType.DMA((3, capacity)),
        ],
        compiler_params=params(50 * 1024 * 1024),
        name="apply",
    )(mine, arrived, root_left[0], root_right[0])
    returned = lax.all_to_all(reply, "dp", split_axis=0, concat_axis=0, tiled=True)

    sums, slot_grads = lax.optimization_barrier((sums, slot_grads))
    sums = sums + swap(sums, 8)
    gram_left = jnp.einsum("sik,sjk->sij", slot_grads, slot_grads, preferred_element_type=jnp.float32)
    gram_right = jnp.einsum("ski,skj->sij", slot_grads, slot_grads, preferred_element_type=jnp.float32)
    new_left = stat_decay * stats_left[0] + coef * gram_left
    new_right = stat_decay * stats_right[0] + coef * gram_right

    direction = pl.pallas_call(
        functools.partial(place_kernel, piece, tiles, col_blocks, n_blocks),
        out_shape=jax.ShapeDtypeStruct((rows_dev, col_width), jnp.bfloat16),
        in_specs=[smem, vmem, vmem],
        out_specs=hbm,
        scratch_shapes=[
            pltpu.VMEM((rows_dev, col_width), jnp.bfloat16),
            pltpu.SemaphoreType.DMA((row_blocks // 2,)),
        ],
        compiler_params=params(),
        name="place",
    )(where, sums, returned)
    return (direction, new_moment, new_left[None], new_right[None])


def solution(mesh):
    in_specs = (
        P("dp", "mp"),
        P("dp", "mp"),
        P("mp", None),
        P("mp", "dp", None, None),
        P("mp", "dp", None, None),
        P("mp", "dp", None, None),
        P("mp", "dp", None, None),
    )
    out_specs = (P("dp", "mp"), P("dp", "mp"), P("mp", "dp", None, None), P("mp", "dp", None, None))
    return jax.shard_map(
        per_device, mesh=mesh, in_specs=in_specs, out_specs=out_specs, check_vma=False
    )
```

time: 93.1 us -> 85.6 us (0.919)
  waiting for transfers between devices: 52.2 us -> 35.9 us
  starting transfers between devices: 19.3 us -> 32.8 us
  Pallas kernels: 10.8 us -> 8.26 us
  local copies, waits for them, and re-layouts: 2.09 us -> 0.1 us
    ppermute x0 -> x7, waiting for transfers between devices: none -> 31.1 us  [swap(): return lax.ppermute(value, 'dp', pairs)]
    all_to_all x1, waiting for transfers between devices: 25.4 us -> 0.34 us  [per_device(): lax.all_to_all(reply, 'dp', split_axis=0, concat_axis=0, tiled=True)]
    all_to_all x1, waiting for transfers between devices: 26.8 us -> 4.46 us  [per_device(): lax.all_to_all(outgoing, 'dp', split_axis=0, concat_axis=0, tiled=True)]
    ppermute x0 -> x7, starting transfers between devices: none -> 13.6 us  [swap(): return lax.ppermute(value, 'dp', pairs)]
    dot_general x1, matrix products: 3.9 us -> 2.18 us  [per_device(): jnp.einsum('ski,skj->sij', slot_grads, slot_grads, preferred_element_type...]
    dot_general x1, matrix products: 2.09 us -> 3.7 us  [per_device(): jnp.einsum('sik,sjk->sij', slot_grads, slot_grads, preferred_element_type...]
    unnamed x12 -> x10, local copies, waits for them, and re-layouts: 1.39 us -> 0.02 us
    pallas_call x1, Pallas kernels: 5.55 us -> 4.59 us  [per_device(): pl.pallas_call(functools.partial(apply_kernel, tiles), out_shape=(jax.Sha...]
  transfers between devices with their start and end apart: 2 -> 9, of which waited for: 2 -> 8; matrix products, arithmetic and copies ran while one was open for 8% -> 9% of each run, Pallas kernels for 0% -> 0%
where the time goes in v2:
time: 85.6 us; the launch traced here: 85.3 us
  waiting for transfers between devices  35.9 us (42%)
  starting transfers between devices  32.8 us (38%)
  Pallas kernels  8.26 us (10%)
  matrix products  5.88 us (7%)
  other arithmetic  1.58 us (2%)
    ppermute x7, waiting for transfers between devices, swap(): return lax.ppermute(value, 'dp', pairs)  31.1 us
    ppermute x7, starting transfers between devices, swap(): return lax.ppermute(value, 'dp', pairs)  13.6 us
    all_to_all x1, starting transfers between devices, per_device(): lax.all_to_all(outgoing, 'dp', split_axis=0, concat_axis=0, tiled=True)  13 us
    all_to_all x1, starting transfers between devices, per_device(): lax.all_to_all(reply, 'dp', split_axis=0, concat_axis=0, tiled=True)  6.21 us
    pallas_call x1, Pallas kernels, per_device(): pl.pallas_call(functools.partial(apply_kernel, tiles), out_shape=(jax.Sha...  4.59 us
    all_to_all x1, waiting for transfers between devices, per_device(): lax.all_to_all(outgoing, 'dp', split_axis=0, concat_axis=0, tiled=True)  4.46 us
    dot_general x1, matrix products, per_device(): jnp.einsum('sik,sjk->sij', slot_grads, slot_grads, preferred_element_type...  3.7 us
    pallas_call x1, Pallas kernels, per_device(): pl.pallas_call(functools.partial(route_kernel, piece, tiles, col_blocks,...  2.22 us
  transfers between devices with their start and end apart: 9, of which 8 were waited for; matrix products, arithmetic and copies ran while one was open for 9% of the time, Pallas kernels for 0%

profile of v2, /device:TPU:1, one launch (start us, length us, event | category | flops | bytes accessed | tf_op | source)
XLA Modules:
  0.0 85.3 jit_solution(14429809274238386635)
XLA Ops:
  0.6 0.0 copy-start.3
  0.6 0.0 copy-start.4
  0.7 2.2 %route.1 = (bf16[64,8,8,128]{3,2,1,0:T(8,128)(2,1)}, s32[2,56]{1,0:T(2,128)}, s32[2]{0:T(128)}) custom-call(s32[1,56]{1,0:T(1,128)} %owner_hbm.1, bf16[64,3584]{1,0:T(8,128)(2,1)} %grads_hbm.1), custom_call_target="tpu_custom_call" | custom-call | tf_op jit(solution)/shard_map/route/pallas_call | solution.py:151
  2.9 13.0 %all-to-all-start = ((bf16[64,8,8,128]{3,2,1,0:T(8,128)(2,1)}), bf16[64,8,8,128]{3,2,1,0:T(8,128)(2,1)S(1)}, u32[]{:S(2)}, u32[]{:S(2)}) async-start(bf16[64,8,8,128]{3,2,1,0:T(8,128)(2,1)} %get-tuple-element.14), calls=%async_computation | async-start | bytes 2097152 | tf_op jit(solution)/shard_map/all_to_all | solution.py:169
  15.9 0.0 copy-done.3
  15.9 0.0 copy-done.4
  15.9 0.0 copy-start.1
  15.9 1.4 %fusion.2 = (f32[64,3584]{1,0:T(8,128)S(1)}, f32[64,3584]{1,0:T(8,128)}) fusion(bf16[64,3584]{1,0:T(8,128)(2,1)S(1)} %copy-done.3, f32[64,3584]{1,0:T(8,128)S(1)} %copy-done.4), kind=kLoop, calls=%fused_computation.6 | loop fusion | flops 1835008 | bytes 3211264 | tf_op jit(solution)/shard_map/mul | solution.py:175
  17.3 0.2 reduce_sum.9
  17.5 0.1 reshape_reshape.3
  17.6 0.5 collective-permute-start
  18.0 0.8 collective-permute-done
  18.9 1.3 %collective-permute-start.1 = (f32[1,56]{1,0:T(1,128)S(1)}, f32[1,56]{1,0:T(1,128)S(1)}, u32[]{:S(2)}, u32[]{:S(2)}) collective-permute-start(f32[1,56]{1,0:T(1,128)S(1)} %add.39), channel_id=1, source_target_pairs={{0,64},{4,68},{8,72},{12,76},{16,80},{20,84},{24,88},{28,92},{32,9... | collective-permute-start | bytes 680 | tf_op jit(solution)/shard_map/ppermute | solution.py:129
  20.2 1.4 %collective-permute-done.1 = f32[1,56]{1,0:T(1,128)S(1)} collective-permute-done((f32[1,56]{1,0:T(1,128)S(1)}, f32[1,56]{1,0:T(1,128)S(1)}, u32[]{:S(2)}, u32[]{:S(2)}) %collective-permute-start.1) | collective-permute-done | bytes 256 | tf_op jit(solution)/shard_map/ppermute | solution.py:129
  21.6 2.9 %collective-permute-start.2 = (f32[1,56]{1,0:T(1,128)S(1)}, f32[1,56]{1,0:T(1,128)S(1)}, u32[]{:S(2)}, u32[]{:S(2)}) collective-permute-start(f32[1,56]{1,0:T(1,128)S(1)} %add.40), channel_id=1, source_target_pairs={{0,128},{4,132},{8,136},{12,140},{16,144},{20,148},{24,152},{28,15... | collective-permute-start | bytes 680 | tf_op jit(solution)/shard_map/ppermute | solution.py:129
  24.5 1.3 %collective-permute-done.2 = f32[1,56]{1,0:T(1,128)S(1)} collective-permute-done((f32[1,56]{1,0:T(1,128)S(1)}, f32[1,56]{1,0:T(1,128)S(1)}, u32[]{:S(2)}, u32[]{:S(2)}) %collective-permute-start.2) | collective-permute-done | bytes 256 | tf_op jit(solution)/shard_map/ppermute | solution.py:129
  25.8 3.1 %collective-permute-start.5 = (f32[1,56]{1,0:T(1,128)S(1)}, f32[1,56]{1,0:T(1,128)S(1)}, u32[]{:S(2)}, u32[]{:S(2)}) collective-permute-start(f32[1,56]{1,0:T(1,128)S(1)} %add.41), channel_id=1, source_target_pairs={{0,24},{4,28},{8,16},{12,20},{16,8},{20,12},{24,0},{28,4},{32,56},... | collective-permute-start | bytes 680 | tf_op jit(solution)/shard_map/ppermute | solution.py:129
  28.8 0.0 collective-permute-start.4
  28.8 0.5 collective-permute-start.3
  29.3 10.3 %collective-permute-done.5 = f32[1,56]{1,0:T(1,128)S(1)} collective-permute-done((f32[1,56]{1,0:T(1,128)S(1)}, f32[1,56]{1,0:T(1,128)S(1)}, u32[]{:S(2)}, u32[]{:S(2)}) %collective-permute-start.5) | collective-permute-done | bytes 256 | tf_op jit(solution)/shard_map/ppermute | solution.py:129
  39.6 0.0 collective-permute-done.4
  39.6 0.4 collective-permute-done.3
  40.0 4.5 %all-to-all-done.arrived = bf16[64,8,8,128]{3,2,1,0:T(8,128)(2,1)S(1)} async-done(((bf16[64,8,8,128]{3,2,1,0:T(8,128)(2,1)}), bf16[64,8,8,128]{3,2,1,0:T(8,128)(2,1)S(1)}, u32[]{:S(2)}, u32[]{:S(2)}) %all-to-all-start) | async-done | bytes 1048608 | tf_op jit(solution)/shard_map/all_to_all | solution.py:169
  44.5 0.0 copy-done.1
  44.5 4.6 %apply.1 = (bf16[64,8,8,128]{3,2,1,0:T(8,128)(2,1)}, bf16[2,512,512]{2,1,0:T(8,128)(2,1)S(1)}) custom-call(s32[2]{0:T(128)S(1)} %copy-done.1, bf16[64,8,8,128]{3,2,1,0:T(8,128)(2,1)S(1)} %all-to-all-done.arrived, bf16[2,512,512]{2,1,0:T(8,128)(2,1)} %bitcast.20, bf16[2,512,512]{2,1,0:T(8,128)(2,1)} %bitcast.21), custom_call_target="tpu_custom_call" | custom-call | tf_op jit(solution)/shard_map/apply/pallas_call | solution.py:183
  49.1 6.2 %all-to-all-start.1 = ((bf16[64,8,8,128]{3,2,1,0:T(8,128)(2,1)}), bf16[64,8,8,128]{3,2,1,0:T(8,128)(2,1)S(1)}, u32[]{:S(2)}, u32[]{:S(2)}) async-start(bf16[64,8,8,128]{3,2,1,0:T(8,128)(2,1)} %get-tuple-element.20), calls=%async_computation.1 | async-start | bytes 2097152 | tf_op jit(solution)/shard_map/all_to_all | solution.py:200
  55.3 0.0 copy-start.2
  55.3 5.4 %collective-permute-start.6 = (f32[1,56]{1,0:T(1,128)S(1)}, f32[1,56]{1,0:T(1,128)S(1)}, u32[]{:S(2)}, u32[]{:S(2)}) collective-permute-start(f32[1,56]{1,0:T(1,128)S(1)} %add_add_fusion), channel_id=1, source_target_pairs={{0,32},{4,36},{8,40},{12,44},{16,48},{20,52},{24,56},{28,60},{32,0... | collective-permute-start | bytes 680 | tf_op jit(solution)/shard_map/ppermute | solution.py:129
  60.7 3.7 %fusion.1 = f32[1,2,512,512]{3,2,1,0:T(8,128)} fusion(f32[1,2,512,512]{3,2,1,0:T(8,128)} %param.10, bf16[2,512,512]{2,1,0:T(8,128)(2,1)S(1)} %get-tuple-element.21), kind=kOutput, calls=%fused_computation.3 | convolution fusion | flops 538443776 | bytes 5242880 | tf_op jit(solution)/shard_map/sik,sjk->sij/dot_general | solution.py:204
  64.4 0.0 copy-done.2
  64.4 0.0 copy-start
  64.4 2.2 %fusion = f32[1,2,512,512]{3,2,1,0:T(8,128)} fusion(f32[1,2,512,512]{3,2,1,0:T(8,128)S(1)} %copy-done.2, bf16[2,512,512]{2,1,0:T(8,128)(2,1)S(1)} %get-tuple-element.21), kind=kOutput, calls=%fused_computation.1 | convolution fusion | flops 538443776 | bytes 5242880 | tf_op jit(solution)/shard_map/ski,skj->sij/dot_general | solution.py:205
  66.6 16.9 %collective-permute-done.6 = f32[1,56]{1,0:T(1,128)S(1)} collective-permute-done((f32[1,56]{1,0:T(1,128)S(1)}, f32[1,56]{1,0:T(1,128)S(1)}, u32[]{:S(2)}, u32[]{:S(2)}) %collective-permute-start.6) | collective-permute-done | bytes 256 | tf_op jit(solution)/shard_map/ppermute | solution.py:129
  83.5 0.3 all-to-all-done.1.back_ref
  83.8 0.0 copy-done
  83.9 1.4 %place.1 = bf16[64,3584]{1,0:T(8,128)(2,1)} custom-call(s32[2,56]{1,0:T(2,128)S(1)} %copy-done, f32[1,56]{1,0:T(1,128)S(1)} %add.45.sums_ref, bf16[64,8,8,128]{3,2,1,0:T(8,128)(2,1)S(1)} %all-to-all-done.1.back_ref), custom_call_target="tpu_custom_call" | custom-call | tf_op jit(solution)/shard_map/place/pallas_call | solution.py:209
  (5 shorter events, 0.0 us)
Async XLA Ops:
  0.6 15.3 %copy-start.3 = (bf16[64,3584]{1,0:T(8,128)(2,1)S(1)}, bf16[64,3584]{1,0:T(8,128)(2,1)}, u32[]{:S(2)}) copy-start(bf16[64,3584]{1,0:T(8,128)(2,1)} %grads_hbm.1) | copy-start | bytes 1376260
  0.6 15.3 %copy-start.4 = (f32[64,3584]{1,0:T(8,128)S(1)}, f32[64,3584]{1,0:T(8,128)}, u32[]{:S(2)}) copy-start(f32[64,3584]{1,0:T(8,128)} %param.8) | copy-start | bytes 2752516
  2.9 41.6 %all-to-all-start = ((bf16[64,8,8,128]{3,2,1,0:T(8,128)(2,1)}), bf16[64,8,8,128]{3,2,1,0:T(8,128)(2,1)S(1)}, u32[]{:S(2)}, u32[]{:S(2)}) async-start(bf16[64,8,8,128]{3,2,1,0:T(8,128)(2,1)} %get-tuple-element.14), calls=%async_computation | async-start | bytes 2097152 | tf_op jit(solution)/shard_map/all_to_all | solution.py:169
  15.9 28.6 %copy-start.1 = (s32[2]{0:T(128)S(1)}, s32[2]{0:T(128)}, u32[]{:S(2)}) copy-start(s32[2]{0:T(128)} %get-tuple-element.16.mine_ref) | copy-start | bytes 28
  17.6 1.3 %collective-permute-start = (f32[1,56]{1,0:T(1,128)S(1)}, f32[1,56]{1,0:T(1,128)S(1)}, u32[]{:S(2)}, u32[]{:S(2)}) collective-permute-start(f32[1,56]{1,0:T(1,128)S(1)} %reshape_reshape.3), channel_id=1, source_target_pairs={{0,4},{4,0},{8,12},{12,8},{16,20},{20,16},{24,28},{28,24},{32,36},... | collective-permute-start | bytes 680 | tf_op jit(solution)/shard_map/ppermute | solution.py:129
  18.9 2.7 %collective-permute-start.1 = (f32[1,56]{1,0:T(1,128)S(1)}, f32[1,56]{1,0:T(1,128)S(1)}, u32[]{:S(2)}, u32[]{:S(2)}) collective-permute-start(f32[1,56]{1,0:T(1,128)S(1)} %add.39), channel_id=1, source_target_pairs={{0,64},{4,68},{8,72},{12,76},{16,80},{20,84},{24,88},{28,92},{32,9... | collective-permute-start | bytes 680 | tf_op jit(solution)/shard_map/ppermute | solution.py:129
  21.6 4.2 %collective-permute-start.2 = (f32[1,56]{1,0:T(1,128)S(1)}, f32[1,56]{1,0:T(1,128)S(1)}, u32[]{:S(2)}, u32[]{:S(2)}) collective-permute-start(f32[1,56]{1,0:T(1,128)S(1)} %add.40), channel_id=1, source_target_pairs={{0,128},{4,132},{8,136},{12,140},{16,144},{20,148},{24,152},{28,15... | collective-permute-start | bytes 680 | tf_op jit(solution)/shard_map/ppermute | solution.py:129
  25.8 13.8 %collective-permute-start.5 = (f32[1,56]{1,0:T(1,128)S(1)}, f32[1,56]{1,0:T(1,128)S(1)}, u32[]{:S(2)}, u32[]{:S(2)}) collective-permute-start(f32[1,56]{1,0:T(1,128)S(1)} %add.41), channel_id=1, source_target_pairs={{0,24},{4,28},{8,16},{12,20},{16,8},{20,12},{24,0},{28,4},{32,56},... | collective-permute-start | bytes 680 | tf_op jit(solution)/shard_map/ppermute | solution.py:129
  28.8 10.7 %collective-permute-start.4 = (f32[1,56]{1,0:T(1,128)S(1)}, f32[1,56]{1,0:T(1,128)S(1)}, u32[]{:S(2)}, u32[]{:S(2)}) collective-permute-start(f32[1,56]{1,0:T(1,128)S(1)} %add.41), channel_id=1, source_target_pairs={{0,16},{4,20},{8,24},{12,28},{16,0},{20,4},{24,8},{28,12},{32,48},... | collective-permute-start | bytes 680 | tf_op jit(solution)/shard_map/ppermute | solution.py:129
  28.8 11.1 %collective-permute-start.3 = (f32[1,56]{1,0:T(1,128)S(1)}, f32[1,56]{1,0:T(1,128)S(1)}, u32[]{:S(2)}, u32[]{:S(2)}) collective-permute-start(f32[1,56]{1,0:T(1,128)S(1)} %add.41), channel_id=1, source_target_pairs={{0,8},{4,12},{8,0},{12,4},{16,24},{20,28},{24,16},{28,20},{32,40},... | collective-permute-start | bytes 680 | tf_op jit(solution)/shard_map/ppermute | solution.py:129
  49.1 34.8 %all-to-all-start.1 = ((bf16[64,8,8,128]{3,2,1,0:T(8,128)(2,1)}), bf16[64,8,8,128]{3,2,1,0:T(8,128)(2,1)S(1)}, u32[]{:S(2)}, u32[]{:S(2)}) async-start(bf16[64,8,8,128]{3,2,1,0:T(8,128)(2,1)} %get-tuple-element.20), calls=%async_computation.1 | async-start | bytes 2097152 | tf_op jit(solution)/shard_map/all_to_all | solution.py:200
  55.3 9.1 %copy-start.2 = (f32[1,2,512,512]{3,2,1,0:T(8,128)S(1)}, f32[1,2,512,512]{3,2,1,0:T(8,128)}, u32[]{:S(2)}) copy-start(f32[1,2,512,512]{3,2,1,0:T(8,128)} %param.11) | copy-start | bytes 6291460
  55.3 28.2 %collective-permute-start.6 = (f32[1,56]{1,0:T(1,128)S(1)}, f32[1,56]{1,0:T(1,128)S(1)}, u32[]{:S(2)}, u32[]{:S(2)}) collective-permute-start(f32[1,56]{1,0:T(1,128)S(1)} %add_add_fusion), channel_id=1, source_target_pairs={{0,32},{4,36},{8,40},{12,44},{16,48},{20,52},{24,56},{28,60},{32,0... | collective-permute-start | bytes 680 | tf_op jit(solution)/shard_map/ppermute | solution.py:129
  64.4 19.5 %copy-start = (s32[2,56]{1,0:T(2,128)S(1)}, s32[2,56]{1,0:T(2,128)}, u32[]{:S(2)}) copy-start(s32[2,56]{1,0:T(2,128)} %get-tuple-element.13.where_ref) | copy-start | bytes 1348

commit v3 on v2

--- a/solution.py
+++ b/solution.py
@@ -55,15 +55,13 @@
                     out_ref[o, s * tiles + j] = part[:, j * LANES:(j + 1) * LANES]
 
 
-def apply_kernel(tiles, mine_ref, arrived, left_hbm, right_hbm, reply_hbm, slots, left, right, reply, sems):
+def apply_kernel(tiles, mine_ref, arrived, left, right_hbm, spare_hbm, reply_hbm, slots, right, reply, sems):
     owner_count, _, piece, _ = arrived.shape
     capacity, size, _ = slots.shape
-    loads = []
-    for s in range(capacity):
-        loads.append(pltpu.make_async_copy(left_hbm.at[s], left.at[s], sems.at[0, s]))
-        loads.append(pltpu.make_async_copy(right_hbm.at[s], right.at[s], sems.at[1, s]))
+    loads = [pltpu.make_async_copy(right_hbm.at[s], right.at[s], sems.at[0, s]) for s in range(capacity)]
     for load in loads:
         load.start()
+
     def gather(s):
         cols = [arrived[:, s * tiles + j].astype(jnp.float32).reshape(size, LANES) for j in range(tiles)]
         grad = jnp.concatenate(cols, axis=1)
@@ -81,17 +79,16 @@
         for j in range(tiles):
             part = unit[:, j * LANES:(j + 1) * LANES].reshape(owner_count, piece, LANES)
             reply[s, :, j] = part.astype(jnp.bfloat16)
-        store = pltpu.make_async_copy(reply.at[s], reply_hbm.at[:, pl.ds(s * tiles, tiles)], sems.at[2, s])
+        store = pltpu.make_async_copy(reply.at[s], reply_hbm.at[:, pl.ds(s * tiles, tiles)], sems.at[1, s])
         store.start()
         return store
 
     stores = []
     gather(0)
-    loads[0].wait()
     applied = first(0)
     for s in range(1, capacity):
         gather(s)
-    for load in loads[1:]:
+    for load in loads:
         load.wait()
     for s in range(capacity):
         precond = second(s, applied)
@@ -186,17 +183,17 @@
             jax.ShapeDtypeStruct((owner_count, capacity * tiles, piece, LANES), jnp.bfloat16),
             jax.ShapeDtypeStruct((capacity, block_size, block_size), jnp.bfloat16),
         ),
-        in_specs=[smem, vmem, hbm, hbm],
+        in_specs=[smem, vmem, vmem, hbm, hbm],
         out_specs=(hbm, vmem),
         scratch_shapes=[
             pltpu.VMEM((capacity, block_size, block_size), jnp.bfloat16),
-            pltpu.VMEM((capacity, block_size, block_size), jnp.bfloat16),
             pltpu.VMEM((capacity, owner_count, tiles, piece, LANES), jnp.bfloat16),
-            pltpu.SemaphoreType.DMA((3, capacity)),
+            pltpu.SemaphoreType.DMA((2, capacity)),
         ],
-        compiler_params=params(50 * 1024 * 1024),
+        input_output_aliases={4: 0},
+        compiler_params=params(49 * 1024 * 1024),
         name="apply",
-    )(mine, arrived, root_left[0], root_right[0])
+    )(mine, arrived, root_left[0], root_right[0], outgoing)
     returned = lax.all_to_all(reply, "dp", split_axis=0, concat_axis=0, tiled=True)
 
     sums, slot_grads = lax.optimization_barrier((sums, slot_grads))

time: 85.6 us -> 85.2 us (level)
  other arithmetic: 1.58 us -> 2.85 us
  waiting for transfers between devices: 35.9 us -> 34.7 us
    mul x1, other arithmetic: 1.39 us -> 2.66 us  [per_device(): adam * adam]
    ppermute x7, waiting for transfers between devices: 31.1 us -> 29.9 us  [swap(): return lax.ppermute(value, 'dp', pairs)]
  transfers between devices with their start and end apart: 9 -> 9, of which waited for: 8 -> 8; matrix products, arithmetic and copies ran while one was open for 9% -> 10% of each run, Pallas kernels for 0% -> 0%
where the time goes in v3:
time: 85.2 us; the launch traced here: 84.8 us
  waiting for transfers between devices  34.7 us (41%)
  starting transfers between devices  32.8 us (38%)
  Pallas kernels  7.79 us (9%)
  matrix products  5.89 us (7%)
  other arithmetic  2.85 us (3%)
    ppermute x7, waiting for transfers between devices, swap(): return lax.ppermute(value, 'dp', pairs)  29.9 us
    ppermute x7, starting transfers between devices, swap(): return lax.ppermute(value, 'dp', pairs)  13.6 us
    all_to_all x1, starting transfers between devices, per_device(): lax.all_to_all(outgoing, 'dp', split_axis=0, concat_axis=0, tiled=True)  13 us
    all_to_all x1, starting transfers between devices, per_device(): lax.all_to_all(reply, 'dp', split_axis=0, concat_axis=0, tiled=True)  6.22 us
    all_to_all x1, waiting for transfers between devices, per_device(): lax.all_to_all(outgoing, 'dp', split_axis=0, concat_axis=0, tiled=True)  4.46 us
    pallas_call x1, Pallas kernels, per_device(): pl.pallas_call(functools.partial(apply_kernel, tiles), out_shape=(jax.Sha...  4.16 us
    dot_general x1, matrix products, per_device(): jnp.einsum('sik,sjk->sij', slot_grads, slot_grads, preferred_element_type...  3.7 us
    mul x1, other arithmetic, per_device(): adam * adam  2.66 us
  transfers between devices with their start and end apart: 9, of which 8 were waited for; matrix products, arithmetic and copies ran while one was open for 10% of the time, Pallas kernels for 0%

profile of v3, /device:TPU:1, one launch (start us, length us, event | category | flops | bytes accessed | tf_op | source)
XLA Modules:
  0.0 84.8 jit_solution(13942363336707375868)
XLA Ops:
  0.6 0.0 copy-start.4
  0.6 2.2 %route.1 = (bf16[64,8,8,128]{3,2,1,0:T(8,128)(2,1)}, s32[2,56]{1,0:T(2,128)}, s32[2]{0:T(128)}) custom-call(s32[1,56]{1,0:T(1,128)} %owner_hbm.1, bf16[64,3584]{1,0:T(8,128)(2,1)} %grads_hbm.1), custom_call_target="tpu_custom_call" | custom-call | tf_op jit(solution)/shard_map/route/pallas_call | solution.py:148
  2.8 13.0 %all-to-all-start = ((bf16[64,8,8,128]{3,2,1,0:T(8,128)(2,1)}), bf16[64,8,8,128]{3,2,1,0:T(8,128)(2,1)S(1)}, u32[]{:S(2)}, u32[]{:S(2)}) async-start(bf16[64,8,8,128]{3,2,1,0:T(8,128)(2,1)} %get-tuple-element.14.spare_hbm), calls=%async_computation | async-start | bytes 2097152 | tf_op jit(solution)/shard_map/all_to_all | solution.py:166
  15.8 0.0 copy-done.4
  15.8 0.0 copy-start
  15.9 0.0 copy-start.2
  15.9 2.7 %fusion.2 = (f32[64,3584]{1,0:T(8,128)S(1)}, f32[64,3584]{1,0:T(8,128)}) fusion(bf16[64,3584]{1,0:T(8,128)(2,1)S(1)} %copy-done.4, f32[64,3584]{1,0:T(8,128)} %param.8), kind=kLoop, calls=%fused_computation.6 | loop fusion | flops 1835008 | bytes 3211264 | tf_op jit(solution)/shard_map/mul | solution.py:172
  18.5 0.2 reduce_sum.9
  18.7 0.1 reshape_reshape.3
  18.8 0.5 collective-permute-start
  19.3 0.8 collective-permute-done
  20.1 1.3 %collective-permute-start.1 = (f32[1,56]{1,0:T(1,128)S(1)}, f32[1,56]{1,0:T(1,128)S(1)}, u32[]{:S(2)}, u32[]{:S(2)}) collective-permute-start(f32[1,56]{1,0:T(1,128)S(1)} %add.39), channel_id=1, source_target_pairs={{0,64},{4,68},{8,72},{12,76},{16,80},{20,84},{24,88},{28,92},{32,9... | collective-permute-start | bytes 680 | tf_op jit(solution)/shard_map/ppermute | solution.py:126
  21.4 1.4 %collective-permute-done.1 = f32[1,56]{1,0:T(1,128)S(1)} collective-permute-done((f32[1,56]{1,0:T(1,128)S(1)}, f32[1,56]{1,0:T(1,128)S(1)}, u32[]{:S(2)}, u32[]{:S(2)}) %collective-permute-start.1) | collective-permute-done | bytes 256 | tf_op jit(solution)/shard_map/ppermute | solution.py:126
  22.8 2.8 %collective-permute-start.2 = (f32[1,56]{1,0:T(1,128)S(1)}, f32[1,56]{1,0:T(1,128)S(1)}, u32[]{:S(2)}, u32[]{:S(2)}) collective-permute-start(f32[1,56]{1,0:T(1,128)S(1)} %add.40), channel_id=1, source_target_pairs={{0,128},{4,132},{8,136},{12,140},{16,144},{20,148},{24,152},{28,15... | collective-permute-start | bytes 680 | tf_op jit(solution)/shard_map/ppermute | solution.py:126
  25.7 1.3 %collective-permute-done.2 = f32[1,56]{1,0:T(1,128)S(1)} collective-permute-done((f32[1,56]{1,0:T(1,128)S(1)}, f32[1,56]{1,0:T(1,128)S(1)}, u32[]{:S(2)}, u32[]{:S(2)}) %collective-permute-start.2) | collective-permute-done | bytes 256 | tf_op jit(solution)/shard_map/ppermute | solution.py:126
  27.0 3.0 %collective-permute-start.5 = (f32[1,56]{1,0:T(1,128)S(1)}, f32[1,56]{1,0:T(1,128)S(1)}, u32[]{:S(2)}, u32[]{:S(2)}) collective-permute-start(f32[1,56]{1,0:T(1,128)S(1)} %add.41), channel_id=1, source_target_pairs={{0,24},{4,28},{8,16},{12,20},{16,8},{20,12},{24,0},{28,4},{32,56},... | collective-permute-start | bytes 680 | tf_op jit(solution)/shard_map/ppermute | solution.py:126
  30.1 0.0 collective-permute-start.4
  30.1 0.5 collective-permute-start.3
  30.6 9.0 %collective-permute-done.5 = f32[1,56]{1,0:T(1,128)S(1)} collective-permute-done((f32[1,56]{1,0:T(1,128)S(1)}, f32[1,56]{1,0:T(1,128)S(1)}, u32[]{:S(2)}, u32[]{:S(2)}) %collective-permute-start.5) | collective-permute-done | bytes 256 | tf_op jit(solution)/shard_map/ppermute | solution.py:126
  39.5 0.0 collective-permute-done.4
  39.5 0.4 collective-permute-done.3
  40.0 4.5 %all-to-all-done.arrived = bf16[64,8,8,128]{3,2,1,0:T(8,128)(2,1)S(1)} async-done(((bf16[64,8,8,128]{3,2,1,0:T(8,128)(2,1)}), bf16[64,8,8,128]{3,2,1,0:T(8,128)(2,1)S(1)}, u32[]{:S(2)}, u32[]{:S(2)}) %all-to-all-start) | async-done | bytes 1048608 | tf_op jit(solution)/shard_map/all_to_all | solution.py:166
  44.4 0.0 copy-done
  44.4 0.0 copy-done.2
  44.4 4.2 %apply.1 = (bf16[64,8,8,128]{3,2,1,0:T(8,128)(2,1)}, bf16[2,512,512]{2,1,0:T(8,128)(2,1)S(1)}) custom-call(s32[2]{0:T(128)S(1)} %copy-done.2, bf16[64,8,8,128]{3,2,1,0:T(8,128)(2,1)S(1)} %all-to-all-done.arrived, bf16[2,512,512]{2,1,0:T(8,128)(2,1)S(1)} %bitcast.19, bf16[2,512,512]{2,1,0:T(8,128)(2,1)} %bitcast.21, ...), custom_call_target="tpu_custom_call", output_to_operand_aliasing={{0}: (4, {})} | custom-call | tf_op jit(solution)/shard_map/apply/pallas_call | solution.py:180
  48.6 6.2 %all-to-all-start.1 = ((bf16[64,8,8,128]{3,2,1,0:T(8,128)(2,1)}), bf16[64,8,8,128]{3,2,1,0:T(8,128)(2,1)S(1)}, u32[]{:S(2)}, u32[]{:S(2)}) async-start(bf16[64,8,8,128]{3,2,1,0:T(8,128)(2,1)} %get-tuple-element.20), calls=%async_computation.1 | async-start | bytes 2097152 | tf_op jit(solution)/shard_map/all_to_all | solution.py:197
  54.8 0.0 copy-start.3
  54.8 5.4 %collective-permute-start.6 = (f32[1,56]{1,0:T(1,128)S(1)}, f32[1,56]{1,0:T(1,128)S(1)}, u32[]{:S(2)}, u32[]{:S(2)}) collective-permute-start(f32[1,56]{1,0:T(1,128)S(1)} %add_add_fusion), channel_id=1, source_target_pairs={{0,32},{4,36},{8,40},{12,44},{16,48},{20,52},{24,56},{28,60},{32,0... | collective-permute-start | bytes 680 | tf_op jit(solution)/shard_map/ppermute | solution.py:126
  60.2 3.7 %fusion.1 = f32[1,2,512,512]{3,2,1,0:T(8,128)} fusion(f32[1,2,512,512]{3,2,1,0:T(8,128)} %param.10, bf16[2,512,512]{2,1,0:T(8,128)(2,1)S(1)} %get-tuple-element.21), kind=kOutput, calls=%fused_computation.3 | convolution fusion | flops 538443776 | bytes 5242880 | tf_op jit(solution)/shard_map/sik,sjk->sij/dot_general | solution.py:201
  63.9 0.0 copy-done.3
  63.9 0.0 copy-start.1
  63.9 2.2 %fusion = f32[1,2,512,512]{3,2,1,0:T(8,128)} fusion(f32[1,2,512,512]{3,2,1,0:T(8,128)S(1)} %copy-done.3, bf16[2,512,512]{2,1,0:T(8,128)(2,1)S(1)} %get-tuple-element.21), kind=kOutput, calls=%fused_computation.1 | convolution fusion | flops 538443776 | bytes 5242880 | tf_op jit(solution)/shard_map/ski,skj->sij/dot_general | solution.py:202
  66.1 16.9 %collective-permute-done.6 = f32[1,56]{1,0:T(1,128)S(1)} collective-permute-done((f32[1,56]{1,0:T(1,128)S(1)}, f32[1,56]{1,0:T(1,128)S(1)}, u32[]{:S(2)}, u32[]{:S(2)}) %collective-permute-start.6) | collective-permute-done | bytes 256 | tf_op jit(solution)/shard_map/ppermute | solution.py:126
  83.0 0.3 all-to-all-done.1.back_ref
  83.4 0.0 copy-done.1
  83.4 1.4 %place.1 = bf16[64,3584]{1,0:T(8,128)(2,1)} custom-call(s32[2,56]{1,0:T(2,128)S(1)} %copy-done.1, f32[1,56]{1,0:T(1,128)S(1)} %add.45.sums_ref, bf16[64,8,8,128]{3,2,1,0:T(8,128)(2,1)S(1)} %all-to-all-done.1.back_ref), custom_call_target="tpu_custom_call" | custom-call | tf_op jit(solution)/shard_map/place/pallas_call | solution.py:206
  (5 shorter events, 0.0 us)
Async XLA Ops:
  0.6 15.2 %copy-start.4 = (bf16[64,3584]{1,0:T(8,128)(2,1)S(1)}, bf16[64,3584]{1,0:T(8,128)(2,1)}, u32[]{:S(2)}) copy-start(bf16[64,3584]{1,0:T(8,128)(2,1)} %grads_hbm.1) | copy-start | bytes 1376260
  2.8 41.6 %all-to-all-start = ((bf16[64,8,8,128]{3,2,1,0:T(8,128)(2,1)}), bf16[64,8,8,128]{3,2,1,0:T(8,128)(2,1)S(1)}, u32[]{:S(2)}, u32[]{:S(2)}) async-start(bf16[64,8,8,128]{3,2,1,0:T(8,128)(2,1)} %get-tuple-element.14.spare_hbm), calls=%async_computation | async-start | bytes 2097152 | tf_op jit(solution)/shard_map/all_to_all | solution.py:166
  15.8 28.6 %copy-start = (bf16[1,2,512,512]{3,2,1,0:T(8,128)(2,1)S(1)}, bf16[1,2,512,512]{3,2,1,0:T(8,128)(2,1)}, u32[]{:S(2)}) copy-start(bf16[1,2,512,512]{3,2,1,0:T(8,128)(2,1)} %param.12) | copy-start | bytes 3145732
  15.9 28.6 %copy-start.2 = (s32[2]{0:T(128)S(1)}, s32[2]{0:T(128)}, u32[]{:S(2)}) copy-start(s32[2]{0:T(128)} %get-tuple-element.16.mine_ref) | copy-start | bytes 28
  18.8 1.3 %collective-permute-start = (f32[1,56]{1,0:T(1,128)S(1)}, f32[1,56]{1,0:T(1,128)S(1)}, u32[]{:S(2)}, u32[]{:S(2)}) collective-permute-start(f32[1,56]{1,0:T(1,128)S(1)} %reshape_reshape.3), channel_id=1, source_target_pairs={{0,4},{4,0},{8,12},{12,8},{16,20},{20,16},{24,28},{28,24},{32,36},... | collective-permute-start | bytes 680 | tf_op jit(solution)/shard_map/ppermute | solution.py:126
  20.1 2.7 %collective-permute-start.1 = (f32[1,56]{1,0:T(1,128)S(1)}, f32[1,56]{1,0:T(1,128)S(1)}, u32[]{:S(2)}, u32[]{:S(2)}) collective-permute-start(f32[1,56]{1,0:T(1,128)S(1)} %add.39), channel_id=1, source_target_pairs={{0,64},{4,68},{8,72},{12,76},{16,80},{20,84},{24,88},{28,92},{32,9... | collective-permute-start | bytes 680 | tf_op jit(solution)/shard_map/ppermute | solution.py:126
  22.8 4.2 %collective-permute-start.2 = (f32[1,56]{1,0:T(1,128)S(1)}, f32[1,56]{1,0:T(1,128)S(1)}, u32[]{:S(2)}, u32[]{:S(2)}) collective-permute-start(f32[1,56]{1,0:T(1,128)S(1)} %add.40), channel_id=1, source_target_pairs={{0,128},{4,132},{8,136},{12,140},{16,144},{20,148},{24,152},{28,15... | collective-permute-start | bytes 680 | tf_op jit(solution)/shard_map/ppermute | solution.py:126
  27.0 12.5 %collective-permute-start.5 = (f32[1,56]{1,0:T(1,128)S(1)}, f32[1,56]{1,0:T(1,128)S(1)}, u32[]{:S(2)}, u32[]{:S(2)}) collective-permute-start(f32[1,56]{1,0:T(1,128)S(1)} %add.41), channel_id=1, source_target_pairs={{0,24},{4,28},{8,16},{12,20},{16,8},{20,12},{24,0},{28,4},{32,56},... | collective-permute-start | bytes 680 | tf_op jit(solution)/shard_map/ppermute | solution.py:126
  30.1 9.5 %collective-permute-start.4 = (f32[1,56]{1,0:T(1,128)S(1)}, f32[1,56]{1,0:T(1,128)S(1)}, u32[]{:S(2)}, u32[]{:S(2)}) collective-permute-start(f32[1,56]{1,0:T(1,128)S(1)} %add.41), channel_id=1, source_target_pairs={{0,16},{4,20},{8,24},{12,28},{16,0},{20,4},{24,8},{28,12},{32,48},... | collective-permute-start | bytes 680 | tf_op jit(solution)/shard_map/ppermute | solution.py:126
  30.1 9.9 %collective-permute-start.3 = (f32[1,56]{1,0:T(1,128)S(1)}, f32[1,56]{1,0:T(1,128)S(1)}, u32[]{:S(2)}, u32[]{:S(2)}) collective-permute-start(f32[1,56]{1,0:T(1,128)S(1)} %add.41), channel_id=1, source_target_pairs={{0,8},{4,12},{8,0},{12,4},{16,24},{20,28},{24,16},{28,20},{32,40},... | collective-permute-start | bytes 680 | tf_op jit(solution)/shard_map/ppermute | solution.py:126
  48.6 34.8 %all-to-all-start.1 = ((bf16[64,8,8,128]{3,2,1,0:T(8,128)(2,1)}), bf16[64,8,8,128]{3,2,1,0:T(8,128)(2,1)S(1)}, u32[]{:S(2)}, u32[]{:S(2)}) async-start(bf16[64,8,8,128]{3,2,1,0:T(8,128)(2,1)} %get-tuple-element.20), calls=%async_computation.1 | async-start | bytes 2097152 | tf_op jit(solution)/shard_map/all_to_all | solution.py:197
  54.8 9.1 %copy-start.3 = (f32[1,2,512,512]{3,2,1,0:T(8,128)S(1)}, f32[1,2,512,512]{3,2,1,0:T(8,128)}, u32[]{:S(2)}) copy-start(f32[1,2,512,512]{3,2,1,0:T(8,128)} %param.11) | copy-start | bytes 6291460
  54.8 28.2 %collective-permute-start.6 = (f32[1,56]{1,0:T(1,128)S(1)}, f32[1,56]{1,0:T(1,128)S(1)}, u32[]{:S(2)}, u32[]{:S(2)}) collective-permute-start(f32[1,56]{1,0:T(1,128)S(1)} %add_add_fusion), channel_id=1, source_target_pairs={{0,32},{4,36},{8,40},{12,44},{16,48},{20,52},{24,56},{28,60},{32,0... | collective-permute-start | bytes 680 | tf_op jit(solution)/shard_map/ppermute | solution.py:126
  63.9 19.5 %copy-start.1 = (s32[2,56]{1,0:T(2,128)S(1)}, s32[2,56]{1,0:T(2,128)}, u32[]{:S(2)}) copy-start(s32[2,56]{1,0:T(2,128)} %get-tuple-element.13.where_ref) | copy-start | bytes 1348

commit v4 on v3

--- a/solution.py
+++ b/solution.py
@@ -55,17 +55,19 @@
                     out_ref[o, s * tiles + j] = part[:, j * LANES:(j + 1) * LANES]
 
 
-def apply_kernel(tiles, mine_ref, arrived, left, right_hbm, spare_hbm, reply_hbm, slots, right, reply, sems):
+def apply_kernel(tiles, mine_hbm, arrived, left, right_hbm, spare_hbm, reply_hbm, slots, right, reply, mine_ref, mine_sem, sems):
     owner_count, _, piece, _ = arrived.shape
     capacity, size, _ = slots.shape
     loads = [pltpu.make_async_copy(right_hbm.at[s], right.at[s], sems.at[0, s]) for s in range(capacity)]
     for load in loads:
         load.start()
+    listing = pltpu.make_async_copy(mine_hbm, mine_ref, mine_sem)
+    listing.start()
 
     def gather(s):
         cols = [arrived[:, s * tiles + j].astype(jnp.float32).reshape(size, LANES) for j in range(tiles)]
         grad = jnp.concatenate(cols, axis=1)
-        slots[s] = jnp.where(mine_ref[s] >= 0, grad, 0.0).astype(jnp.bfloat16)
+        slots[s] = grad.astype(jnp.bfloat16)
 
     def first(s):
         return jnp.dot(left[s], slots[s], preferred_element_type=jnp.float32).astype(jnp.bfloat16)
@@ -95,6 +97,12 @@
         if s + 1 < capacity:
             applied = first(s + 1)
         stores.append(send(s, precond))
+    listing.wait()
+    for s in range(capacity):
+        @pl.when(mine_ref[s] < 0)
+        def _():
+            slots[s] = jnp.zeros(slots.shape[1:], slots.dtype)
+
     for store in stores:
         store.wait()
 
@@ -183,11 +191,13 @@
             jax.ShapeDtypeStruct((owner_count, capacity * tiles, piece, LANES), jnp.bfloat16),
             jax.ShapeDtypeStruct((capacity, block_size, block_size), jnp.bfloat16),
         ),
-        in_specs=[smem, vmem, vmem, hbm, hbm],
+        in_specs=[hbm, vmem, vmem, hbm, hbm],
         out_specs=(hbm, vmem),
         scratch_shapes=[
             pltpu.VMEM((capacity, block_size, block_size), jnp.bfloat16),
             pltpu.VMEM((capacity, owner_count, tiles, piece, LANES), jnp.bfloat16),
+            pltpu.SMEM((capacity,), jnp.int32),
+            pltpu.SemaphoreType.DMA(()),
             pltpu.SemaphoreType.DMA((2, capacity)),
         ],
         input_output_aliases={4: 0},

time: 85.2 us -> 84.7 us (level)
  no operation moved by 1% of the time
where the time goes in v4:
time: 84.7 us; the launch traced here: 84.3 us
  waiting for transfers between devices  34.7 us (41%)
  starting transfers between devices  32.8 us (39%)
  Pallas kernels  7.25 us (9%)
  matrix products  5.89 us (7%)
  other arithmetic  2.85 us (3%)
    ppermute x7, waiting for transfers between devices, swap(): return lax.ppermute(value, 'dp', pairs)  29.9 us
    ppermute x7, starting transfers between devices, swap(): return lax.ppermute(value, 'dp', pairs)  13.6 us
    all_to_all x1, starting transfers between devices, per_device(): lax.all_to_all(outgoing, 'dp', split_axis=0, concat_axis=0, tiled=True)  13 us
    all_to_all x1, starting transfers between devices, per_device(): lax.all_to_all(reply, 'dp', split_axis=0, concat_axis=0, tiled=True)  6.22 us
    all_to_all x1, waiting for transfers between devices, per_device(): lax.all_to_all(outgoing, 'dp', split_axis=0, concat_axis=0, tiled=True)  4.46 us
    dot_general x1, matrix products, per_device(): jnp.einsum('sik,sjk->sij', slot_grads, slot_grads, preferred_element_type...  3.71 us
    pallas_call x1, Pallas kernels, per_device(): pl.pallas_call(functools.partial(apply_kernel, tiles), out_shape=(jax.Sha...  3.62 us
    mul x1, other arithmetic, per_device(): adam * adam  2.66 us
  transfers between devices with their start and end apart: 9, of which 8 were waited for; matrix products, arithmetic and copies ran while one was open for 10% of the time, Pallas kernels for 0%

profile of v4, /device:TPU:1, one launch (start us, length us, event | category | flops | bytes accessed | tf_op | source)
XLA Modules:
  0.0 84.3 jit_solution(9085677378585362862)
XLA Ops:
  0.6 0.0 copy-start.4
  0.6 2.2 %route.1 = (bf16[64,8,8,128]{3,2,1,0:T(8,128)(2,1)}, s32[2,56]{1,0:T(2,128)}, s32[2]{0:T(128)}) custom-call(s32[1,56]{1,0:T(1,128)} %owner_hbm.1, bf16[64,3584]{1,0:T(8,128)(2,1)} %grads_hbm.1), custom_call_target="tpu_custom_call" | custom-call | tf_op jit(solution)/shard_map/route/pallas_call | solution.py:156
  2.8 13.0 %all-to-all-start = ((bf16[64,8,8,128]{3,2,1,0:T(8,128)(2,1)}), bf16[64,8,8,128]{3,2,1,0:T(8,128)(2,1)S(1)}, u32[]{:S(2)}, u32[]{:S(2)}) async-start(bf16[64,8,8,128]{3,2,1,0:T(8,128)(2,1)} %get-tuple-element.14.spare_hbm), calls=%async_computation | async-start | bytes 2097152 | tf_op jit(solution)/shard_map/all_to_all | solution.py:174
  15.8 0.0 copy-done.4
  15.8 0.0 copy-start
  15.9 0.0 copy-start.2
  15.9 2.7 %fusion.2 = (f32[64,3584]{1,0:T(8,128)S(1)}, f32[64,3584]{1,0:T(8,128)}) fusion(bf16[64,3584]{1,0:T(8,128)(2,1)S(1)} %copy-done.4, f32[64,3584]{1,0:T(8,128)} %param.8), kind=kLoop, calls=%fused_computation.6 | loop fusion | flops 1835008 | bytes 3211264 | tf_op jit(solution)/shard_map/mul | solution.py:180
  18.5 0.2 reduce_sum.9
  18.7 0.1 reshape_reshape.3
  18.8 0.5 collective-permute-start
  19.3 0.8 collective-permute-done
  20.1 1.3 %collective-permute-start.1 = (f32[1,56]{1,0:T(1,128)S(1)}, f32[1,56]{1,0:T(1,128)S(1)}, u32[]{:S(2)}, u32[]{:S(2)}) collective-permute-start(f32[1,56]{1,0:T(1,128)S(1)} %add.39), channel_id=1, source_target_pairs={{0,64},{4,68},{8,72},{12,76},{16,80},{20,84},{24,88},{28,92},{32,9... | collective-permute-start | bytes 680 | tf_op jit(solution)/shard_map/ppermute | solution.py:134
  21.4 1.4 %collective-permute-done.1 = f32[1,56]{1,0:T(1,128)S(1)} collective-permute-done((f32[1,56]{1,0:T(1,128)S(1)}, f32[1,56]{1,0:T(1,128)S(1)}, u32[]{:S(2)}, u32[]{:S(2)}) %collective-permute-start.1) | collective-permute-done | bytes 256 | tf_op jit(solution)/shard_map/ppermute | solution.py:134
  22.8 2.8 %collective-permute-start.2 = (f32[1,56]{1,0:T(1,128)S(1)}, f32[1,56]{1,0:T(1,128)S(1)}, u32[]{:S(2)}, u32[]{:S(2)}) collective-permute-start(f32[1,56]{1,0:T(1,128)S(1)} %add.40), channel_id=1, source_target_pairs={{0,128},{4,132},{8,136},{12,140},{16,144},{20,148},{24,152},{28,15... | collective-permute-start | bytes 680 | tf_op jit(solution)/shard_map/ppermute | solution.py:134
  25.7 1.3 %collective-permute-done.2 = f32[1,56]{1,0:T(1,128)S(1)} collective-permute-done((f32[1,56]{1,0:T(1,128)S(1)}, f32[1,56]{1,0:T(1,128)S(1)}, u32[]{:S(2)}, u32[]{:S(2)}) %collective-permute-start.2) | collective-permute-done | bytes 256 | tf_op jit(solution)/shard_map/ppermute | solution.py:134
  27.0 3.0 %collective-permute-start.5 = (f32[1,56]{1,0:T(1,128)S(1)}, f32[1,56]{1,0:T(1,128)S(1)}, u32[]{:S(2)}, u32[]{:S(2)}) collective-permute-start(f32[1,56]{1,0:T(1,128)S(1)} %add.41), channel_id=1, source_target_pairs={{0,24},{4,28},{8,16},{12,20},{16,8},{20,12},{24,0},{28,4},{32,56},... | collective-permute-start | bytes 680 | tf_op jit(solution)/shard_map/ppermute | solution.py:134
  30.1 0.0 collective-permute-start.4
  30.1 0.5 collective-permute-start.3
  30.6 9.0 %collective-permute-done.5 = f32[1,56]{1,0:T(1,128)S(1)} collective-permute-done((f32[1,56]{1,0:T(1,128)S(1)}, f32[1,56]{1,0:T(1,128)S(1)}, u32[]{:S(2)}, u32[]{:S(2)}) %collective-permute-start.5) | collective-permute-done | bytes 256 | tf_op jit(solution)/shard_map/ppermute | solution.py:134
  39.5 0.0 collective-permute-done.4
  39.5 0.4 collective-permute-done.3
  40.0 4.5 %all-to-all-done.arrived = bf16[64,8,8,128]{3,2,1,0:T(8,128)(2,1)S(1)} async-done(((bf16[64,8,8,128]{3,2,1,0:T(8,128)(2,1)}), bf16[64,8,8,128]{3,2,1,0:T(8,128)(2,1)S(1)}, u32[]{:S(2)}, u32[]{:S(2)}) %all-to-all-start) | async-done | bytes 1048608 | tf_op jit(solution)/shard_map/all_to_all | solution.py:174
  44.4 0.0 copy-done
  44.4 0.0 copy-done.2
  44.4 3.6 %apply.1 = (bf16[64,8,8,128]{3,2,1,0:T(8,128)(2,1)}, bf16[2,512,512]{2,1,0:T(8,128)(2,1)S(1)}) custom-call(s32[2]{0:T(128)S(1)} %copy-done.2, bf16[64,8,8,128]{3,2,1,0:T(8,128)(2,1)S(1)} %all-to-all-done.arrived, bf16[2,512,512]{2,1,0:T(8,128)(2,1)S(1)} %bitcast.19, bf16[2,512,512]{2,1,0:T(8,128)(2,1)} %bitcast.21, ...), custom_call_target="tpu_custom_call", output_to_operand_aliasing={{0}: (4, {})} | custom-call | tf_op jit(solution)/shard_map/apply/pallas_call | solution.py:188
  48.0 6.2 %all-to-all-start.1 = ((bf16[64,8,8,128]{3,2,1,0:T(8,128)(2,1)}), bf16[64,8,8,128]{3,2,1,0:T(8,128)(2,1)S(1)}, u32[]{:S(2)}, u32[]{:S(2)}) async-start(bf16[64,8,8,128]{3,2,1,0:T(8,128)(2,1)} %get-tuple-element.20), calls=%async_computation.1 | async-start | bytes 2097152 | tf_op jit(solution)/shard_map/all_to_all | solution.py:207
  54.3 0.0 copy-start.3
  54.3 5.4 %collective-permute-start.6 = (f32[1,56]{1,0:T(1,128)S(1)}, f32[1,56]{1,0:T(1,128)S(1)}, u32[]{:S(2)}, u32[]{:S(2)}) collective-permute-start(f32[1,56]{1,0:T(1,128)S(1)} %add_add_fusion), channel_id=1, source_target_pairs={{0,32},{4,36},{8,40},{12,44},{16,48},{20,52},{24,56},{28,60},{32,0... | collective-permute-start | bytes 680 | tf_op jit(solution)/shard_map/ppermute | solution.py:134
  59.7 3.7 %fusion.1 = f32[1,2,512,512]{3,2,1,0:T(8,128)} fusion(f32[1,2,512,512]{3,2,1,0:T(8,128)} %param.10, bf16[2,512,512]{2,1,0:T(8,128)(2,1)S(1)} %get-tuple-element.21), kind=kOutput, calls=%fused_computation.3 | convolution fusion | flops 538443776 | bytes 5242880 | tf_op jit(solution)/shard_map/sik,sjk->sij/dot_general | solution.py:211
  63.4 0.0 copy-done.3
  63.4 0.0 copy-start.1
  63.4 2.2 %fusion = f32[1,2,512,512]{3,2,1,0:T(8,128)} fusion(f32[1,2,512,512]{3,2,1,0:T(8,128)S(1)} %copy-done.3, bf16[2,512,512]{2,1,0:T(8,128)(2,1)S(1)} %get-tuple-element.21), kind=kOutput, calls=%fused_computation.1 | convolution fusion | flops 538443776 | bytes 5242880 | tf_op jit(solution)/shard_map/ski,skj->sij/dot_general | solution.py:212
  65.6 16.9 %collective-permute-done.6 = f32[1,56]{1,0:T(1,128)S(1)} collective-permute-done((f32[1,56]{1,0:T(1,128)S(1)}, f32[1,56]{1,0:T(1,128)S(1)}, u32[]{:S(2)}, u32[]{:S(2)}) %collective-permute-start.6) | collective-permute-done | bytes 256 | tf_op jit(solution)/shard_map/ppermute | solution.py:134
  82.5 0.3 all-to-all-done.1.back_ref
  82.8 0.0 copy-done.1
  82.9 1.4 %place.1 = bf16[64,3584]{1,0:T(8,128)(2,1)} custom-call(s32[2,56]{1,0:T(2,128)S(1)} %copy-done.1, f32[1,56]{1,0:T(1,128)S(1)} %add.45.sums_ref, bf16[64,8,8,128]{3,2,1,0:T(8,128)(2,1)S(1)} %all-to-all-done.1.back_ref), custom_call_target="tpu_custom_call" | custom-call | tf_op jit(solution)/shard_map/place/pallas_call | solution.py:216
  (5 shorter events, 0.0 us)
Async XLA Ops:
  0.6 15.2 %copy-start.4 = (bf16[64,3584]{1,0:T(8,128)(2,1)S(1)}, bf16[64,3584]{1,0:T(8,128)(2,1)}, u32[]{:S(2)}) copy-start(bf16[64,3584]{1,0:T(8,128)(2,1)} %grads_hbm.1) | copy-start | bytes 1376260
  2.8 41.6 %all-to-all-start = ((bf16[64,8,8,128]{3,2,1,0:T(8,128)(2,1)}), bf16[64,8,8,128]{3,2,1,0:T(8,128)(2,1)S(1)}, u32[]{:S(2)}, u32[]{:S(2)}) async-start(bf16[64,8,8,128]{3,2,1,0:T(8,128)(2,1)} %get-tuple-element.14.spare_hbm), calls=%async_computation | async-start | bytes 2097152 | tf_op jit(solution)/shard_map/all_to_all | solution.py:174
  15.8 28.6 %copy-start = (bf16[1,2,512,512]{3,2,1,0:T(8,128)(2,1)S(1)}, bf16[1,2,512,512]{3,2,1,0:T(8,128)(2,1)}, u32[]{:S(2)}) copy-start(bf16[1,2,512,512]{3,2,1,0:T(8,128)(2,1)} %param.12) | copy-start | bytes 3145732
  15.9 28.6 %copy-start.2 = (s32[2]{0:T(128)S(1)}, s32[2]{0:T(128)}, u32[]{:S(2)}) copy-start(s32[2]{0:T(128)} %get-tuple-element.16.mine_hbm) | copy-start | bytes 28
  18.8 1.3 %collective-permute-start = (f32[1,56]{1,0:T(1,128)S(1)}, f32[1,56]{1,0:T(1,128)S(1)}, u32[]{:S(2)}, u32[]{:S(2)}) collective-permute-start(f32[1,56]{1,0:T(1,128)S(1)} %reshape_reshape.3), channel_id=1, source_target_pairs={{0,4},{4,0},{8,12},{12,8},{16,20},{20,16},{24,28},{28,24},{32,36},... | collective-permute-start | bytes 680 | tf_op jit(solution)/shard_map/ppermute | solution.py:134
  20.1 2.7 %collective-permute-start.1 = (f32[1,56]{1,0:T(1,128)S(1)}, f32[1,56]{1,0:T(1,128)S(1)}, u32[]{:S(2)}, u32[]{:S(2)}) collective-permute-start(f32[1,56]{1,0:T(1,128)S(1)} %add.39), channel_id=1, source_target_pairs={{0,64},{4,68},{8,72},{12,76},{16,80},{20,84},{24,88},{28,92},{32,9... | collective-permute-start | bytes 680 | tf_op jit(solution)/shard_map/ppermute | solution.py:134
  22.8 4.2 %collective-permute-start.2 = (f32[1,56]{1,0:T(1,128)S(1)}, f32[1,56]{1,0:T(1,128)S(1)}, u32[]{:S(2)}, u32[]{:S(2)}) collective-permute-start(f32[1,56]{1,0:T(1,128)S(1)} %add.40), channel_id=1, source_target_pairs={{0,128},{4,132},{8,136},{12,140},{16,144},{20,148},{24,152},{28,15... | collective-permute-start | bytes 680 | tf_op jit(solution)/shard_map/ppermute | solution.py:134
  27.0 12.5 %collective-permute-start.5 = (f32[1,56]{1,0:T(1,128)S(1)}, f32[1,56]{1,0:T(1,128)S(1)}, u32[]{:S(2)}, u32[]{:S(2)}) collective-permute-start(f32[1,56]{1,0:T(1,128)S(1)} %add.41), channel_id=1, source_target_pairs={{0,24},{4,28},{8,16},{12,20},{16,8},{20,12},{24,0},{28,4},{32,56},... | collective-permute-start | bytes 680 | tf_op jit(solution)/shard_map/ppermute | solution.py:134
  30.1 9.5 %collective-permute-start.4 = (f32[1,56]{1,0:T(1,128)S(1)}, f32[1,56]{1,0:T(1,128)S(1)}, u32[]{:S(2)}, u32[]{:S(2)}) collective-permute-start(f32[1,56]{1,0:T(1,128)S(1)} %add.41), channel_id=1, source_target_pairs={{0,16},{4,20},{8,24},{12,28},{16,0},{20,4},{24,8},{28,12},{32,48},... | collective-permute-start | bytes 680 | tf_op jit(solution)/shard_map/ppermute | solution.py:134
  30.1 9.9 %collective-permute-start.3 = (f32[1,56]{1,0:T(1,128)S(1)}, f32[1,56]{1,0:T(1,128)S(1)}, u32[]{:S(2)}, u32[]{:S(2)}) collective-permute-start(f32[1,56]{1,0:T(1,128)S(1)} %add.41), channel_id=1, source_target_pairs={{0,8},{4,12},{8,0},{12,4},{16,24},{20,28},{24,16},{28,20},{32,40},... | collective-permute-start | bytes 680 | tf_op jit(solution)/shard_map/ppermute | solution.py:134
  48.0 34.8 %all-to-all-start.1 = ((bf16[64,8,8,128]{3,2,1,0:T(8,128)(2,1)}), bf16[64,8,8,128]{3,2,1,0:T(8,128)(2,1)S(1)}, u32[]{:S(2)}, u32[]{:S(2)}) async-start(bf16[64,8,8,128]{3,2,1,0:T(8,128)(2,1)} %get-tuple-element.20), calls=%async_computation.1 | async-start | bytes 2097152 | tf_op jit(solution)/shard_map/all_to_all | solution.py:207
  54.3 9.1 %copy-start.3 = (f32[1,2,512,512]{3,2,1,0:T(8,128)S(1)}, f32[1,2,512,512]{3,2,1,0:T(8,128)}, u32[]{:S(2)}) copy-start(f32[1,2,512,512]{3,2,1,0:T(8,128)} %param.11) | copy-start | bytes 6291460
  54.3 28.2 %collective-permute-start.6 = (f32[1,56]{1,0:T(1,128)S(1)}, f32[1,56]{1,0:T(1,128)S(1)}, u32[]{:S(2)}, u32[]{:S(2)}) collective-permute-start(f32[1,56]{1,0:T(1,128)S(1)} %add_add_fusion), channel_id=1, source_target_pairs={{0,32},{4,36},{8,40},{12,44},{16,48},{20,52},{24,56},{28,60},{32,0... | collective-permute-start | bytes 680 | tf_op jit(solution)/shard_map/ppermute | solution.py:134
  63.4 19.5 %copy-start.1 = (s32[2,56]{1,0:T(2,128)S(1)}, s32[2,56]{1,0:T(2,128)}, u32[]{:S(2)}) copy-start(s32[2,56]{1,0:T(2,128)} %get-tuple-element.13.where_ref) | copy-start | bytes 1348

commit v5 on v4

--- a/solution.py
+++ b/solution.py
@@ -180,8 +180,8 @@
         (adam * adam).reshape(row_blocks, piece, col_blocks, block_size), axis=(1, 3)
     ).reshape(n_blocks)
     sums = block_sq.reshape(1, n_blocks)
-    for step in (1, 16, 32):
-        sums = sums + swap(sums, step)
+    sums = sums + swap(sums, 1)
+    sums = sums + swap(sums, 16) + swap(sums, 32) + swap(sums, 48)
     sums = sums + swap(sums, 2) + swap(sums, 4) + swap(sums, 6)
 
     arrived, sums = lax.optimization_barrier((arrived, sums))

time: 84.7 us -> 84.7 us (level)
    ppermute x7 -> x8, waiting for transfers between devices: 29.9 us -> 30.7 us  [swap(): return lax.ppermute(value, 'dp', pairs)]
    ppermute x7 -> x8, starting transfers between devices: 13.6 us -> 12.8 us  [swap(): return lax.ppermute(value, 'dp', pairs)]
  transfers between devices with their start and end apart: 9 -> 10, of which waited for: 8 -> 8; matrix products, arithmetic and copies ran while one was open for 10% -> 10% of each run, Pallas kernels for 0% -> 0%
where the time goes in v5:
time: 84.7 us; the launch traced here: 84.3 us
  waiting for transfers between devices  35.5 us (42%)
  starting transfers between devices  32 us (38%)
  Pallas kernels  7.28 us (9%)
  matrix products  5.89 us (7%)
  other arithmetic  2.84 us (3%)
    ppermute x8, waiting for transfers between devices, swap(): return lax.ppermute(value, 'dp', pairs)  30.7 us
    all_to_all x1, starting transfers between devices, per_device(): lax.all_to_all(outgoing, 'dp', split_axis=0, concat_axis=0, tiled=True)  13 us
    ppermute x8, starting transfers between devices, swap(): return lax.ppermute(value, 'dp', pairs)  12.8 us
    all_to_all x1, starting transfers between devices, per_device(): lax.all_to_all(reply, 'dp', split_axis=0, concat_axis=0, tiled=True)  6.21 us
    all_to_all x1, waiting for transfers between devices, per_device(): lax.all_to_all(outgoing, 'dp', split_axis=0, concat_axis=0, tiled=True)  4.46 us
    dot_general x1, matrix products, per_device(): jnp.einsum('sik,sjk->sij', slot_grads, slot_grads, preferred_element_type...  3.71 us
    pallas_call x1, Pallas kernels, per_device(): pl.pallas_call(functools.partial(apply_kernel, tiles), out_shape=(jax.Sha...  3.63 us
    mul x1, other arithmetic, per_device(): adam * adam  2.66 us
  transfers between devices with their start and end apart: 10, of which 8 were waited for; matrix products, arithmetic and copies ran while one was open for 10% of the time, Pallas kernels for 0%

profile of v5, /device:TPU:1, one launch (start us, length us, event | category | flops | bytes accessed | tf_op | source)
XLA Modules:
  0.0 84.3 jit_solution(7166417262288364359)
XLA Ops:
  0.6 0.0 copy-start.4
  0.6 2.2 %route.1 = (bf16[64,8,8,128]{3,2,1,0:T(8,128)(2,1)}, s32[2,56]{1,0:T(2,128)}, s32[2]{0:T(128)}) custom-call(s32[1,56]{1,0:T(1,128)} %owner_hbm.1, bf16[64,3584]{1,0:T(8,128)(2,1)} %grads_hbm.1), custom_call_target="tpu_custom_call" | custom-call | tf_op jit(solution)/shard_map/route/pallas_call | solution.py:156
  2.8 13.0 %all-to-all-start = ((bf16[64,8,8,128]{3,2,1,0:T(8,128)(2,1)}), bf16[64,8,8,128]{3,2,1,0:T(8,128)(2,1)S(1)}, u32[]{:S(2)}, u32[]{:S(2)}) async-start(bf16[64,8,8,128]{3,2,1,0:T(8,128)(2,1)} %get-tuple-element.14.spare_hbm), calls=%async_computation | async-start | bytes 2097152 | tf_op jit(solution)/shard_map/all_to_all | solution.py:174
  15.9 0.0 copy-done.4
  15.9 0.0 copy-start
  15.9 0.0 copy-start.2
  15.9 2.7 %fusion.2 = (f32[64,3584]{1,0:T(8,128)S(1)}, f32[64,3584]{1,0:T(8,128)}) fusion(bf16[64,3584]{1,0:T(8,128)(2,1)S(1)} %copy-done.4, f32[64,3584]{1,0:T(8,128)} %param.8), kind=kLoop, calls=%fused_computation.6 | loop fusion | flops 1835008 | bytes 3211264 | tf_op jit(solution)/shard_map/mul | solution.py:180
  18.5 0.2 reduce_sum.9
  18.7 0.1 reshape_reshape.3
  18.8 0.5 collective-permute-start
  19.3 0.8 collective-permute-done
  20.1 2.7 %collective-permute-start.3 = (f32[1,56]{1,0:T(1,128)S(1)}, f32[1,56]{1,0:T(1,128)S(1)}, u32[]{:S(2)}, u32[]{:S(2)}) collective-permute-start(f32[1,56]{1,0:T(1,128)S(1)} %add.42), channel_id=1, source_target_pairs={{0,192},{4,196},{8,200},{12,204},{16,208},{20,212},{24,216},{28,22... | collective-permute-start | bytes 680 | tf_op jit(solution)/shard_map/ppermute | solution.py:134
  22.8 0.4 collective-permute-start.2
  23.2 0.2 collective-permute-start.1
  23.4 0.6 collective-permute-done.3
  24.0 3.0 %collective-permute-done.2 = f32[1,56]{1,0:T(1,128)S(1)} collective-permute-done((f32[1,56]{1,0:T(1,128)S(1)}, f32[1,56]{1,0:T(1,128)S(1)}, u32[]{:S(2)}, u32[]{:S(2)}) %collective-permute-start.2) | collective-permute-done | bytes 256 | tf_op jit(solution)/shard_map/ppermute | solution.py:134
  27.0 0.0 collective-permute-done.1
  27.0 3.1 %collective-permute-start.6 = (f32[1,56]{1,0:T(1,128)S(1)}, f32[1,56]{1,0:T(1,128)S(1)}, u32[]{:S(2)}, u32[]{:S(2)}) collective-permute-start(f32[1,56]{1,0:T(1,128)S(1)} %add_add_fusion.1), channel_id=1, source_target_pairs={{0,24},{4,28},{8,16},{12,20},{16,8},{20,12},{24,0},{28,4},{32,56},... | collective-permute-start | bytes 680 | tf_op jit(solution)/shard_map/ppermute | solution.py:134
  30.1 0.0 collective-permute-start.5
  30.1 0.5 collective-permute-start.4
  30.6 8.9 %collective-permute-done.6 = f32[1,56]{1,0:T(1,128)S(1)} collective-permute-done((f32[1,56]{1,0:T(1,128)S(1)}, f32[1,56]{1,0:T(1,128)S(1)}, u32[]{:S(2)}, u32[]{:S(2)}) %collective-permute-start.6) | collective-permute-done | bytes 256 | tf_op jit(solution)/shard_map/ppermute | solution.py:134
  39.6 0.0 collective-permute-done.5
  39.6 0.4 collective-permute-done.4
  40.0 4.5 %all-to-all-done.arrived = bf16[64,8,8,128]{3,2,1,0:T(8,128)(2,1)S(1)} async-done(((bf16[64,8,8,128]{3,2,1,0:T(8,128)(2,1)}), bf16[64,8,8,128]{3,2,1,0:T(8,128)(2,1)S(1)}, u32[]{:S(2)}, u32[]{:S(2)}) %all-to-all-start) | async-done | bytes 1048608 | tf_op jit(solution)/shard_map/all_to_all | solution.py:174
  44.4 0.0 copy-done
  44.4 0.0 copy-done.2
  44.4 3.6 %apply.1 = (bf16[64,8,8,128]{3,2,1,0:T(8,128)(2,1)}, bf16[2,512,512]{2,1,0:T(8,128)(2,1)S(1)}) custom-call(s32[2]{0:T(128)S(1)} %copy-done.2, bf16[64,8,8,128]{3,2,1,0:T(8,128)(2,1)S(1)} %all-to-all-done.arrived, bf16[2,512,512]{2,1,0:T(8,128)(2,1)S(1)} %bitcast.19, bf16[2,512,512]{2,1,0:T(8,128)(2,1)} %bitcast.21, ...), custom_call_target="tpu_custom_call", output_to_operand_aliasing={{0}: (4, {})} | custom-call | tf_op jit(solution)/shard_map/apply/pallas_call | solution.py:188
  48.1 6.2 %all-to-all-start.1 = ((bf16[64,8,8,128]{3,2,1,0:T(8,128)(2,1)}), bf16[64,8,8,128]{3,2,1,0:T(8,128)(2,1)S(1)}, u32[]{:S(2)}, u32[]{:S(2)}) async-start(bf16[64,8,8,128]{3,2,1,0:T(8,128)(2,1)} %get-tuple-element.20), calls=%async_computation.1 | async-start | bytes 2097152 | tf_op jit(solution)/shard_map/all_to_all | solution.py:207
  54.3 0.0 copy-start.3
  54.3 5.4 %collective-permute-start.7 = (f32[1,56]{1,0:T(1,128)S(1)}, f32[1,56]{1,0:T(1,128)S(1)}, u32[]{:S(2)}, u32[]{:S(2)}) collective-permute-start(f32[1,56]{1,0:T(1,128)S(1)} %add_add_fusion), channel_id=1, source_target_pairs={{0,32},{4,36},{8,40},{12,44},{16,48},{20,52},{24,56},{28,60},{32,0... | collective-permute-start | bytes 680 | tf_op jit(solution)/shard_map/ppermute | solution.py:134
  59.7 3.7 %fusion.1 = f32[1,2,512,512]{3,2,1,0:T(8,128)} fusion(f32[1,2,512,512]{3,2,1,0:T(8,128)} %param.10, bf16[2,512,512]{2,1,0:T(8,128)(2,1)S(1)} %get-tuple-element.21), kind=kOutput, calls=%fused_computation.3 | convolution fusion | flops 538443776 | bytes 5242880 | tf_op jit(solution)/shard_map/sik,sjk->sij/dot_general | solution.py:211
  63.4 0.0 copy-done.3
  63.4 0.0 copy-start.1
  63.4 2.2 %fusion = f32[1,2,512,512]{3,2,1,0:T(8,128)} fusion(f32[1,2,512,512]{3,2,1,0:T(8,128)S(1)} %copy-done.3, bf16[2,512,512]{2,1,0:T(8,128)(2,1)S(1)} %get-tuple-element.21), kind=kOutput, calls=%fused_computation.1 | convolution fusion | flops 538443776 | bytes 5242880 | tf_op jit(solution)/shard_map/ski,skj->sij/dot_general | solution.py:212
  65.6 16.9 %collective-permute-done.7 = f32[1,56]{1,0:T(1,128)S(1)} collective-permute-done((f32[1,56]{1,0:T(1,128)S(1)}, f32[1,56]{1,0:T(1,128)S(1)}, u32[]{:S(2)}, u32[]{:S(2)}) %collective-permute-start.7) | collective-permute-done | bytes 256 | tf_op jit(solution)/shard_map/ppermute | solution.py:134
  82.5 0.3 all-to-all-done.1.back_ref
  82.9 0.0 copy-done.1
  82.9 1.4 %place.1 = bf16[64,3584]{1,0:T(8,128)(2,1)} custom-call(s32[2,56]{1,0:T(2,128)S(1)} %copy-done.1, f32[1,56]{1,0:T(1,128)S(1)} %add.49.sums_ref, bf16[64,8,8,128]{3,2,1,0:T(8,128)(2,1)S(1)} %all-to-all-done.1.back_ref), custom_call_target="tpu_custom_call" | custom-call | tf_op jit(solution)/shard_map/place/pallas_call | solution.py:216
  (4 shorter events, 0.0 us)
Async XLA Ops:
  0.6 15.2 %copy-start.4 = (bf16[64,3584]{1,0:T(8,128)(2,1)S(1)}, bf16[64,3584]{1,0:T(8,128)(2,1)}, u32[]{:S(2)}) copy-start(bf16[64,3584]{1,0:T(8,128)(2,1)} %grads_hbm.1) | copy-start | bytes 1376260
  2.8 41.6 %all-to-all-start = ((bf16[64,8,8,128]{3,2,1,0:T(8,128)(2,1)}), bf16[64,8,8,128]{3,2,1,0:T(8,128)(2,1)S(1)}, u32[]{:S(2)}, u32[]{:S(2)}) async-start(bf16[64,8,8,128]{3,2,1,0:T(8,128)(2,1)} %get-tuple-element.14.spare_hbm), calls=%async_computation | async-start | bytes 2097152 | tf_op jit(solution)/shard_map/all_to_all | solution.py:174
  15.9 28.6 %copy-start = (bf16[1,2,512,512]{3,2,1,0:T(8,128)(2,1)S(1)}, bf16[1,2,512,512]{3,2,1,0:T(8,128)(2,1)}, u32[]{:S(2)}) copy-start(bf16[1,2,512,512]{3,2,1,0:T(8,128)(2,1)} %param.12) | copy-start | bytes 3145732
  15.9 28.6 %copy-start.2 = (s32[2]{0:T(128)S(1)}, s32[2]{0:T(128)}, u32[]{:S(2)}) copy-start(s32[2]{0:T(128)} %get-tuple-element.16.mine_hbm) | copy-start | bytes 28
  18.8 1.3 %collective-permute-start = (f32[1,56]{1,0:T(1,128)S(1)}, f32[1,56]{1,0:T(1,128)S(1)}, u32[]{:S(2)}, u32[]{:S(2)}) collective-permute-start(f32[1,56]{1,0:T(1,128)S(1)} %reshape_reshape.3), channel_id=1, source_target_pairs={{0,4},{4,0},{8,12},{12,8},{16,20},{20,16},{24,28},{28,24},{32,36},... | collective-permute-start | bytes 680 | tf_op jit(solution)/shard_map/ppermute | solution.py:134
  20.1 3.9 %collective-permute-start.3 = (f32[1,56]{1,0:T(1,128)S(1)}, f32[1,56]{1,0:T(1,128)S(1)}, u32[]{:S(2)}, u32[]{:S(2)}) collective-permute-start(f32[1,56]{1,0:T(1,128)S(1)} %add.42), channel_id=1, source_target_pairs={{0,192},{4,196},{8,200},{12,204},{16,208},{20,212},{24,216},{28,22... | collective-permute-start | bytes 680 | tf_op jit(solution)/shard_map/ppermute | solution.py:134
  22.8 4.2 %collective-permute-start.2 = (f32[1,56]{1,0:T(1,128)S(1)}, f32[1,56]{1,0:T(1,128)S(1)}, u32[]{:S(2)}, u32[]{:S(2)}) collective-permute-start(f32[1,56]{1,0:T(1,128)S(1)} %add.42), channel_id=1, source_target_pairs={{0,128},{4,132},{8,136},{12,140},{16,144},{20,148},{24,152},{28,15... | collective-permute-start | bytes 680 | tf_op jit(solution)/shard_map/ppermute | solution.py:134
  23.2 3.8 %collective-permute-start.1 = (f32[1,56]{1,0:T(1,128)S(1)}, f32[1,56]{1,0:T(1,128)S(1)}, u32[]{:S(2)}, u32[]{:S(2)}) collective-permute-start(f32[1,56]{1,0:T(1,128)S(1)} %add.42), channel_id=1, source_target_pairs={{0,64},{4,68},{8,72},{12,76},{16,80},{20,84},{24,88},{28,92},{32,9... | collective-permute-start | bytes 680 | tf_op jit(solution)/shard_map/ppermute | solution.py:134
  27.0 12.5 %collective-permute-start.6 = (f32[1,56]{1,0:T(1,128)S(1)}, f32[1,56]{1,0:T(1,128)S(1)}, u32[]{:S(2)}, u32[]{:S(2)}) collective-permute-start(f32[1,56]{1,0:T(1,128)S(1)} %add_add_fusion.1), channel_id=1, source_target_pairs={{0,24},{4,28},{8,16},{12,20},{16,8},{20,12},{24,0},{28,4},{32,56},... | collective-permute-start | bytes 680 | tf_op jit(solution)/shard_map/ppermute | solution.py:134
  30.1 9.4 %collective-permute-start.5 = (f32[1,56]{1,0:T(1,128)S(1)}, f32[1,56]{1,0:T(1,128)S(1)}, u32[]{:S(2)}, u32[]{:S(2)}) collective-permute-start(f32[1,56]{1,0:T(1,128)S(1)} %add_add_fusion.1), channel_id=1, source_target_pairs={{0,16},{4,20},{8,24},{12,28},{16,0},{20,4},{24,8},{28,12},{32,48},... | collective-permute-start | bytes 680 | tf_op jit(solution)/shard_map/ppermute | solution.py:134
  30.1 9.8 %collective-permute-start.4 = (f32[1,56]{1,0:T(1,128)S(1)}, f32[1,56]{1,0:T(1,128)S(1)}, u32[]{:S(2)}, u32[]{:S(2)}) collective-permute-start(f32[1,56]{1,0:T(1,128)S(1)} %add_add_fusion.1), channel_id=1, source_target_pairs={{0,8},{4,12},{8,0},{12,4},{16,24},{20,28},{24,16},{28,20},{32,40},... | collective-permute-start | bytes 680 | tf_op jit(solution)/shard_map/ppermute | solution.py:134
  48.1 34.8 %all-to-all-start.1 = ((bf16[64,8,8,128]{3,2,1,0:T(8,128)(2,1)}), bf16[64,8,8,128]{3,2,1,0:T(8,128)(2,1)S(1)}, u32[]{:S(2)}, u32[]{:S(2)}) async-start(bf16[64,8,8,128]{3,2,1,0:T(8,128)(2,1)} %get-tuple-element.20), calls=%async_computation.1 | async-start | bytes 2097152 | tf_op jit(solution)/shard_map/all_to_all | solution.py:207
  54.3 9.1 %copy-start.3 = (f32[1,2,512,512]{3,2,1,0:T(8,128)S(1)}, f32[1,2,512,512]{3,2,1,0:T(8,128)}, u32[]{:S(2)}) copy-start(f32[1,2,512,512]{3,2,1,0:T(8,128)} %param.11) | copy-start | bytes 6291460
  54.3 28.2 %collective-permute-start.7 = (f32[1,56]{1,0:T(1,128)S(1)}, f32[1,56]{1,0:T(1,128)S(1)}, u32[]{:S(2)}, u32[]{:S(2)}) collective-permute-start(f32[1,56]{1,0:T(1,128)S(1)} %add_add_fusion), channel_id=1, source_target_pairs={{0,32},{4,36},{8,40},{12,44},{16,48},{20,52},{24,56},{28,60},{32,0... | collective-permute-start | bytes 680 | tf_op jit(solution)/shard_map/ppermute | solution.py:134
  63.4 19.5 %copy-start.1 = (s32[2,56]{1,0:T(2,128)S(1)}, s32[2,56]{1,0:T(2,128)}, u32[]{:S(2)}) copy-start(s32[2,56]{1,0:T(2,128)} %get-tuple-element.13.where_ref) | copy-start | bytes 1348
